TPU v7x, 32 devices: a whole 2x2x4 slice. The times are simulated.
32 devices in a mesh: section: 4 (over y, x), dp: 8 (over z, core).
Axes of the slice: x: 2, y: 2, z: 4, core: 2. Of those that a mesh axis runs over, the one named last changes fastest.
Arguments:
- enc_in: bfloat16 [32, 512, 768], P('dp', 'section'), may hold values from -6 to 6
- lengths: int32 [32], P('dp'), may hold values from 40 to 512, as said below
- dec_in: bfloat16 [32, 768], P('dp', 'section'), may hold values from -6 to 6
- gains: bfloat16 [4, 2, 768], P('section'), may hold values from 0.5 to 1.5
- weights: bfloat16 [4, 8, 768, 768], P('section')
- d_out: bfloat16 [32, 768], P('dp', 'section'), may hold values from -6 to 6
Outputs:
- dec_out: bfloat16 [32, 768], P('dp', 'section')
- d_enc_in: bfloat16 [32, 512, 768], P('dp', 'section')
- d_dec_in: bfloat16 [32, 768], P('dp', 'section')
- d_gains: float32 [4, 2, 768], P('section')
- d_weights: float32 [4, 8, 768, 768], P('section')
Inputs may be any that keep to these rules, and one draw needn't show every extreme that they name: Positions below lengths[p] are passage p's tokens, the rest padding; some passage has exactly 512 tokens and some exactly 40.
All inputs are finite; a program needn't handle non-finite values.
Results may differ from a plain program's by a relative error of at most 0.017.
Values may be sent and summed in bfloat16 or wider, within the bound.
A program may use at most 192 MiB of HBM per device.

v0:
```python
import math

import jax
import jax.numpy as jnp
from jax import lax
from jax.sharding import PartitionSpec as P

D = 768
HEADS = 12
HEAD = 64
KEY_BLOCK = 128
MICRO = 4


epsilon = 1e-06
masked_score = -1e30
gelu_coeff = 0.044715


def shortened(value):
    return jax.tree.map(lambda a: a.astype(jnp.bfloat16) if a.dtype == jnp.float32 else a, value)


def from_behind(block, axis, distance):
    devices = range(lax.axis_size(axis))
    route = [(i - distance, i) for i in devices if i - distance in devices]
    return lax.ppermute(block, axis, route)


def gelu_slope(pre_values):
    inner_scale = math.sqrt(2.0 / math.pi)
    tangent = jnp.tanh(
        inner_scale * (pre_values + gelu_coeff * pre_values * pre_values * pre_values)
    )
    return 0.5 * (1.0 + tangent) + 0.5 * pre_values * (1.0 - tangent * tangent) * inner_scale * (
        1.0 + 3.0 * gelu_coeff * pre_values * pre_values
    )


def product(left_side, right_side):
    flattened = left_side.reshape(-1, left_side.shape[-1])
    result = jnp.dot(flattened, right_side, preferred_element_type=jnp.float32)
    return result.reshape(left_side.shape[:-1] + (right_side.shape[1],))


def product_back(left_side, right_side):
    flattened = left_side.reshape(-1, left_side.shape[-1])
    result = lax.dot_general(
        flattened, right_side, (((1,), (1,)), ((), ())), preferred_element_type=jnp.float32
    )
    return result.reshape(left_side.shape[:-1] + (right_side.shape[0],))


def weight_term(left_side, grad_side):
    left_flat = left_side.reshape(-1, left_side.shape[-1])
    grad_flat = grad_side.reshape(-1, grad_side.shape[-1])
    return lax.dot_general(
        left_flat, grad_flat, (((0,), (0,)), ((), ())), preferred_element_type=jnp.float32
    )


def norm_forward(values_in, gain_row):
    inverse = lax.rsqrt(jnp.mean(values_in * values_in, axis=-1, keepdims=True) + epsilon)
    normed = values_in * inverse
    return (normed * gain_row, normed, inverse)


def norm_backward(normed, inverse, gain_row, grad_out):
    scaled = grad_out * gain_row
    grad_in = inverse * (scaled - normed * jnp.mean(scaled * normed, axis=-1, keepdims=True))
    grad_gain = jnp.sum((grad_out * normed).reshape(-1, normed.shape[-1]), axis=0)
    return (grad_in, grad_gain)


def key_scores(queries, key_rows, lengths, block_index):
    key_block = lax.dynamic_slice_in_dim(key_rows, block_index * KEY_BLOCK, KEY_BLOCK, 1)
    scores = jnp.einsum("blhd,bkhd->bhlk", queries, key_block, preferred_element_type=jnp.float32)
    places = block_index * KEY_BLOCK + lax.iota(jnp.int32, KEY_BLOCK)
    is_valid = places[None, :] < lengths[:, None]
    return jnp.where(is_valid[:, None, None, :], scores, masked_score)


def attention_stats(queries, key_rows, lengths, block_count):
    row_shape = (queries.shape[0], HEADS, queries.shape[1])

    def visit_block(block_index, state_in):
        running_max, running_sum = state_in
        scores = key_scores(queries, key_rows, lengths, block_index)
        new_max = jnp.maximum(running_max, jnp.max(scores, axis=-1))
        running_sum = running_sum * jnp.exp(running_max - new_max) + jnp.sum(
            jnp.exp(scores - new_max[..., None]), axis=-1
        )
        return (new_max, running_sum)

    start_state = (
        jnp.full(row_shape, masked_score, jnp.float32),
        jnp.zeros(row_shape, jnp.float32),
    )
    final_max, final_sum = lax.fori_loop(0, block_count, visit_block, start_state)
    return final_max + jnp.log(final_sum)


def attention_mix(queries, key_rows, values, lengths, block_count, log_total):

    def visit_block(block_index, total_mix):
        scores = key_scores(queries, key_rows, lengths, block_index)
        probs_low = jnp.exp(scores - log_total[..., None]).astype(jnp.bfloat16)
        value_block = lax.dynamic_slice_in_dim(values, block_index * KEY_BLOCK, KEY_BLOCK, 1)
        return total_mix + jnp.einsum(
            "bhlk,bkhd->blhd", probs_low, value_block, preferred_element_type=jnp.float32
        )

    return lax.fori_loop(0, block_count, visit_block, jnp.zeros(queries.shape, jnp.float32))


def attention_back(queries, key_rows, values, lengths, block_count, log_total, grad_mix):

    def probs_and_grad(block_index):
        scores = key_scores(queries, key_rows, lengths, block_index)
        probs_full = jnp.exp(scores - log_total[..., None])
        value_block = lax.dynamic_slice_in_dim(values, block_index * KEY_BLOCK, KEY_BLOCK, 1)
        grad_probs = jnp.einsum(
            "blhd,bkhd->bhlk", grad_mix, value_block, preferred_element_type=jnp.float32
        )
        return (probs_full, grad_probs)

    def visit_sum(block_index, running):
        probs_full, grad_probs = probs_and_grad(block_index)
        return running + jnp.sum(probs_full * grad_probs, axis=-1)

    centre = lax.fori_loop(0, block_count, visit_sum, jnp.zeros(log_total.shape, jnp.float32))

    def visit_grad(block_index, state_in):
        grad_queries, grad_keys, grad_values = state_in
        probs_full, grad_probs = probs_and_grad(block_index)
        grad_scores = (probs_full * (grad_probs - centre[..., None])).astype(jnp.bfloat16)
        key_block = lax.dynamic_slice_in_dim(key_rows, block_index * KEY_BLOCK, KEY_BLOCK, 1)
        grad_queries = grad_queries + jnp.einsum(
            "bhlk,bkhd->blhd", grad_scores, key_block, preferred_element_type=jnp.float32
        )
        key_part = jnp.einsum(
            "bhlk,blhd->bkhd", grad_scores, queries, preferred_element_type=jnp.float32
        )
        value_part = jnp.einsum(
            "bhlk,blhd->bkhd",
            probs_full.astype(jnp.bfloat16),
            grad_mix,
            preferred_element_type=jnp.float32,
        )
        grad_keys = lax.dynamic_update_slice_in_dim(grad_keys, key_part, block_index * KEY_BLOCK, 1)
        grad_values = lax.dynamic_update_slice_in_dim(
            grad_values, value_part, block_index * KEY_BLOCK, 1
        )
        return (grad_queries, grad_keys, grad_values)

    zero_rows = jnp.zeros(queries.shape, jnp.float32)
    return lax.fori_loop(0, block_count, visit_grad, (zero_rows, zero_rows, zero_rows))


def encoder_pieces(enc_rows, lengths, section_weights, gain_rows):
    batch_size, length = (enc_rows.shape[0], enc_rows.shape[1])
    values_in = enc_rows.astype(jnp.float32)
    scaled, normed, inverse = norm_forward(values_in, gain_rows[0].astype(jnp.float32))
    acts_low = scaled.astype(jnp.bfloat16)
    split_shape = (batch_size, length, HEADS, HEAD)
    queries = product(acts_low, section_weights[0]).astype(jnp.bfloat16).reshape(split_shape)
    key_rows = product(acts_low, section_weights[1]).astype(jnp.bfloat16).reshape(split_shape)
    values = product(acts_low, section_weights[2]).astype(jnp.bfloat16).reshape(split_shape)
    block_count = (jnp.max(lengths) + KEY_BLOCK - 1) // KEY_BLOCK
    log_total = attention_stats(queries, key_rows, lengths, block_count)
    mixed = attention_mix(queries, key_rows, values, lengths, block_count, log_total)
    mixed = mixed.astype(jnp.bfloat16).reshape(batch_size, length, D)
    return {
        "values_in": values_in,
        "normed": normed,
        "inverse": inverse,
        "acts_low": acts_low,
        "queries": queries,
        "key_rows": key_rows,
        "values": values,
        "block_count": block_count,
        "log_total": log_total,
        "mixed": mixed,
    }


def feed_pieces(rows_in, section_weights, gain_row):
    values_in = rows_in.astype(jnp.float32).reshape(-1, D)
    scaled, normed, inverse = norm_forward(values_in, gain_row.astype(jnp.float32))
    acts_low = scaled.astype(jnp.bfloat16)
    hidden_pre = jnp.einsum(
        "td,bdf->tbf", acts_low, section_weights[0:4], preferred_element_type=jnp.float32
    )
    hidden_low = jax.nn.gelu(hidden_pre, approximate=True).astype(jnp.bfloat16)
    return (values_in, normed, inverse, acts_low, hidden_pre, hidden_low)


def feed_forward(rows_in, section_weights, gain_row):
    values_in, normed, inverse, acts_low, hidden_pre, hidden_low = feed_pieces(
        rows_in, section_weights, gain_row
    )
    result = values_in + jnp.einsum(
        "tbf,bfd->td", hidden_low, section_weights[4:8], preferred_element_type=jnp.float32
    )
    return result.astype(jnp.bfloat16).reshape(rows_in.shape)


def feed_backward(rows_in, section_weights, gain_row, grad_rows):
    values_in, normed, inverse, acts_low, hidden_pre, hidden_low = feed_pieces(
        rows_in, section_weights, gain_row
    )
    grad_flat = grad_rows.reshape(-1, D)
    term_out = jnp.einsum("tbf,td->bfd", hidden_low, grad_flat, preferred_element_type=jnp.float32)
    grad_hidden = jnp.einsum(
        "td,bfd->tbf", grad_flat, section_weights[4:8], preferred_element_type=jnp.float32
    )
    grad_pre = (grad_hidden * gelu_slope(hidden_pre)).astype(jnp.bfloat16)
    term_in = jnp.einsum("td,tbf->bdf", acts_low, grad_pre, preferred_element_type=jnp.float32)
    grad_acts = jnp.einsum(
        "tbf,bdf->td", grad_pre, section_weights[0:4], preferred_element_type=jnp.float32
    )
    grad_in, grad_gain = norm_backward(normed, inverse, gain_row.astype(jnp.float32), grad_acts)
    grad_total = (grad_flat.astype(jnp.float32) + grad_in).reshape(rows_in.shape)
    return (grad_total, jnp.concatenate([term_in, term_out], axis=0), grad_gain)


def cross_pieces(enc_rows, start_rows, lengths, section_weights, gain_rows):
    batch_size, length = (enc_rows.shape[0], enc_rows.shape[1])
    start_in = start_rows.astype(jnp.float32)
    scaled_self, normed_self, inverse_self = norm_forward(
        start_in, gain_rows[0].astype(jnp.float32)
    )
    self_acts = scaled_self.astype(jnp.bfloat16)
    self_values = product(self_acts, section_weights[0]).astype(jnp.bfloat16)
    middle = start_in + product(self_values, section_weights[1])
    scaled_cross, normed_cross, inverse_cross = norm_forward(
        middle, gain_rows[1].astype(jnp.float32)
    )
    cross_acts = scaled_cross.astype(jnp.bfloat16)
    queries = (
        product(cross_acts, section_weights[2])
        .astype(jnp.bfloat16)
        .reshape(batch_size, HEADS, HEAD)
    )
    key_rows = (
        product(enc_rows, section_weights[3])
        .astype(jnp.bfloat16)
        .reshape(batch_size, length, HEADS, HEAD)
    )
    values = (
        product(enc_rows, section_weights[4])
        .astype(jnp.bfloat16)
        .reshape(batch_size, length, HEADS, HEAD)
    )
    scores = jnp.einsum("bhd,blhd->bhl", queries, key_rows, preferred_element_type=jnp.float32)
    is_valid = lax.iota(jnp.int32, length)[None, :] < lengths[:, None]
    probs_full = jax.nn.softmax(jnp.where(is_valid[:, None, :], scores, masked_score), axis=-1)
    probs_low = probs_full.astype(jnp.bfloat16)
    mixed = jnp.einsum("bhl,blhd->bhd", probs_low, values, preferred_element_type=jnp.float32)
    mixed = mixed.astype(jnp.bfloat16).reshape(batch_size, D)
    return {
        "normed_self": normed_self,
        "inverse_self": inverse_self,
        "self_acts": self_acts,
        "self_values": self_values,
        "middle": middle,
        "normed_cross": normed_cross,
        "inverse_cross": inverse_cross,
        "cross_acts": cross_acts,
        "queries": queries,
        "key_rows": key_rows,
        "values": values,
        "probs_full": probs_full,
        "probs_low": probs_low,
        "mixed": mixed,
    }


def forward_zero(big_in, small_in, length_part, section_weights, gain_rows):
    pieces = encoder_pieces(big_in, length_part, section_weights, gain_rows)
    result = pieces["values_in"] + product(pieces["mixed"], section_weights[3])
    return (result.astype(jnp.bfloat16), jnp.zeros_like(small_in))


def forward_one(big_in, small_in, length_part, section_weights, gain_rows):
    return (feed_forward(big_in, section_weights, gain_rows[0]), jnp.zeros_like(small_in))


def forward_two(big_in, small_in, length_part, section_weights, gain_rows):
    pieces = cross_pieces(big_in, small_in, length_part, section_weights, gain_rows)
    result = pieces["middle"] + product(pieces["mixed"], section_weights[5])
    return (jnp.zeros_like(big_in), result.astype(jnp.bfloat16))


def forward_three(big_in, small_in, length_part, section_weights, gain_rows):
    return (jnp.zeros_like(big_in), feed_forward(small_in, section_weights, gain_rows[0]))


def backward_zero(big_in, small_in, grad_big, grad_small, length_part, section_weights, gain_rows):
    pieces = encoder_pieces(big_in, length_part, section_weights, gain_rows)
    batch_size, length = (big_in.shape[0], big_in.shape[1])
    term_out = weight_term(pieces["mixed"], grad_big)
    grad_mixed = product_back(grad_big, section_weights[3]).astype(jnp.bfloat16)
    grad_mixed = grad_mixed.reshape(pieces["queries"].shape)
    grad_queries, grad_keys, grad_values = attention_back(
        pieces["queries"],
        pieces["key_rows"],
        pieces["values"],
        length_part,
        pieces["block_count"],
        pieces["log_total"],
        grad_mixed,
    )
    joined = (batch_size, length, D)
    grad_queries = grad_queries.astype(jnp.bfloat16).reshape(joined)
    grad_keys = grad_keys.astype(jnp.bfloat16).reshape(joined)
    grad_values = grad_values.astype(jnp.bfloat16).reshape(joined)
    term_query = weight_term(pieces["acts_low"], grad_queries)
    term_keys = weight_term(pieces["acts_low"], grad_keys)
    term_values = weight_term(pieces["acts_low"], grad_values)
    grad_acts = (
        product_back(grad_queries, section_weights[0])
        + product_back(grad_keys, section_weights[1])
        + product_back(grad_values, section_weights[2])
    )
    grad_in, grad_gain = norm_backward(
        pieces["normed"], pieces["inverse"], gain_rows[0].astype(jnp.float32), grad_acts
    )
    grad_enc = grad_big.astype(jnp.float32) + grad_in
    zero_block = jnp.zeros((D, D), jnp.float32)
    term_stack = jnp.stack(
        [
            term_query,
            term_keys,
            term_values,
            term_out,
            zero_block,
            zero_block,
            zero_block,
            zero_block,
        ]
    )
    gain_stack = jnp.stack([grad_gain, jnp.zeros((D,), jnp.float32)])
    return (
        jnp.zeros_like(big_in),
        jnp.zeros_like(small_in),
        grad_enc,
        jnp.zeros(small_in.shape, jnp.float32),
        term_stack,
        gain_stack,
    )


def backward_one(big_in, small_in, grad_big, grad_small, length_part, section_weights, gain_rows):
    grad_total, term_stack, grad_gain = feed_backward(
        big_in, section_weights, gain_rows[0], grad_big
    )
    gain_stack = jnp.stack([grad_gain, jnp.zeros((D,), jnp.float32)])
    return (
        grad_total.astype(jnp.bfloat16),
        jnp.zeros_like(small_in),
        jnp.zeros(big_in.shape, jnp.float32),
        jnp.zeros(small_in.shape, jnp.float32),
        term_stack,
        gain_stack,
    )


def backward_two(big_in, small_in, grad_big, grad_small, length_part, section_weights, gain_rows):
    pieces = cross_pieces(big_in, small_in, length_part, section_weights, gain_rows)
    batch_size, length = (big_in.shape[0], big_in.shape[1])
    term_out = weight_term(pieces["mixed"], grad_small)
    grad_mixed = (
        product_back(grad_small, section_weights[5])
        .astype(jnp.bfloat16)
        .reshape(batch_size, HEADS, HEAD)
    )
    grad_probs = jnp.einsum(
        "bhd,blhd->bhl", grad_mixed, pieces["values"], preferred_element_type=jnp.float32
    )
    grad_values = jnp.einsum(
        "bhl,bhd->blhd", pieces["probs_low"], grad_mixed, preferred_element_type=jnp.float32
    )
    grad_values = grad_values.astype(jnp.bfloat16).reshape(batch_size, length, D)
    probs_full = pieces["probs_full"]
    grad_scores = probs_full * (
        grad_probs - jnp.sum(probs_full * grad_probs, axis=-1, keepdims=True)
    )
    grad_scores = grad_scores.astype(jnp.bfloat16)
    grad_queries = jnp.einsum(
        "bhl,blhd->bhd", grad_scores, pieces["key_rows"], preferred_element_type=jnp.float32
    )
    grad_queries = grad_queries.astype(jnp.bfloat16).reshape(batch_size, D)
    grad_keys = jnp.einsum(
        "bhl,bhd->blhd", grad_scores, pieces["queries"], preferred_element_type=jnp.float32
    )
    grad_keys = grad_keys.astype(jnp.bfloat16).reshape(batch_size, length, D)
    term_query = weight_term(pieces["cross_acts"], grad_queries)
    term_keys = weight_term(big_in, grad_keys)
    term_values = weight_term(big_in, grad_values)
    grad_enc = product_back(grad_keys, section_weights[3]) + product_back(
        grad_values, section_weights[4]
    )
    grad_cross = product_back(grad_queries, section_weights[2])
    grad_mid_norm, gain_cross = norm_backward(
        pieces["normed_cross"],
        pieces["inverse_cross"],
        gain_rows[1].astype(jnp.float32),
        grad_cross,
    )
    grad_middle = grad_small.astype(jnp.float32) + grad_mid_norm
    middle_low = grad_middle.astype(jnp.bfloat16)
    term_self_out = weight_term(pieces["self_values"], middle_low)
    grad_self_values = product_back(middle_low, section_weights[1]).astype(jnp.bfloat16)
    term_self_values = weight_term(pieces["self_acts"], grad_self_values)
    grad_self = product_back(grad_self_values, section_weights[0])
    grad_start_norm, gain_self = norm_backward(
        pieces["normed_self"], pieces["inverse_self"], gain_rows[0].astype(jnp.float32), grad_self
    )
    grad_start = grad_middle + grad_start_norm
    zero_block = jnp.zeros((D, D), jnp.float32)
    term_stack = jnp.stack(
        [
            term_self_values,
            term_self_out,
            term_query,
            term_keys,
            term_values,
            term_out,
            zero_block,
            zero_block,
        ]
    )
    gain_stack = jnp.stack([gain_self, gain_cross])
    return (
        grad_enc.astype(jnp.bfloat16),
        jnp.zeros_like(small_in),
        jnp.zeros(big_in.shape, jnp.float32),
        grad_start,
        term_stack,
        gain_stack,
    )


def backward_three(big_in, small_in, grad_big, grad_small, length_part, section_weights, gain_rows):
    grad_total, term_stack, grad_gain = feed_backward(
        small_in, section_weights, gain_rows[0], grad_small
    )
    gain_stack = jnp.stack([grad_gain, jnp.zeros((D,), jnp.float32)])
    return (
        jnp.zeros_like(big_in),
        grad_total.astype(jnp.bfloat16),
        jnp.zeros(big_in.shape, jnp.float32),
        jnp.zeros(small_in.shape, jnp.float32),
        term_stack,
        gain_stack,
    )


def local(enc_in, lengths, dec_in, gains, weights, d_out):
    section_index = lax.axis_index("section")
    sections = lax.axis_size("section")
    enc_rows, start_rows, cotangent = (
        lax.all_gather(enc_in, "section", axis=1, tiled=True),
        lax.all_gather(dec_in, "section", axis=1, tiled=True),
        lax.all_gather(d_out, "section", axis=1, tiled=True),
    )
    section_weights = weights[0]
    gain_rows = gains[0]
    per_micro = enc_rows.shape[0] // MICRO
    tick_count = MICRO + sections - 1
    big_zero = jnp.zeros((per_micro,) + enc_rows.shape[1:], jnp.bfloat16)
    small_zero = jnp.zeros((per_micro, start_rows.shape[1]), jnp.bfloat16)
    kept_big = jnp.zeros((MICRO,) + big_zero.shape, jnp.bfloat16)
    kept_small = jnp.zeros((MICRO,) + small_zero.shape, jnp.bfloat16)
    decoded = jnp.zeros(start_rows.shape, jnp.bfloat16)

    def forward_tick(tick_index, state_in):
        recv_big, recv_small, kept_big, kept_small, decoded = state_in
        micro_index = tick_index - section_index
        is_live = (micro_index >= 0) & (micro_index < MICRO)
        slot_index = jnp.clip(micro_index, 0, MICRO - 1)
        first_row = slot_index * per_micro
        enc_part = lax.dynamic_slice_in_dim(enc_rows, first_row, per_micro, 0)
        start_part = lax.dynamic_slice_in_dim(start_rows, first_row, per_micro, 0)
        length_part = lax.dynamic_slice_in_dim(lengths, first_row, per_micro, 0)
        big_in = jnp.where(section_index == 0, enc_part, recv_big)
        small_in = jnp.where(section_index == 2, start_part, recv_small)
        kept_big = lax.dynamic_update_index_in_dim(
            kept_big, jnp.where(is_live, big_in, kept_big[slot_index]), slot_index, 0
        )
        kept_small = lax.dynamic_update_index_in_dim(
            kept_small, jnp.where(is_live, small_in, kept_small[slot_index]), slot_index, 0
        )
        big_out, small_out = lax.switch(
            section_index,
            [forward_zero, forward_one, forward_two, forward_three],
            big_in,
            small_in,
            length_part,
            section_weights,
            gain_rows,
        )
        old_rows = lax.dynamic_slice_in_dim(decoded, first_row, per_micro, 0)
        keep_out = jnp.where(is_live & (section_index == sections - 1), small_out, old_rows)
        decoded = lax.dynamic_update_slice_in_dim(decoded, keep_out, first_row, 0)
        recv_big, recv_small = (
            from_behind(shortened(big_out), "section", 1).astype(big_out.dtype),
            from_behind(shortened(small_out), "section", 1).astype(small_out.dtype),
        )
        return (recv_big, recv_small, kept_big, kept_small, decoded)

    forward_state = lax.fori_loop(
        0, tick_count, forward_tick, (big_zero, small_zero, kept_big, kept_small, decoded)
    )
    kept_big, kept_small, decoded = (forward_state[2], forward_state[3], forward_state[4])
    sum_weights = jnp.zeros((8, D, D), jnp.float32)
    sum_gains = jnp.zeros((2, D), jnp.float32)
    grad_enc_rows = jnp.zeros(enc_rows.shape, jnp.float32)
    grad_start_rows = jnp.zeros(start_rows.shape, jnp.float32)

    def backward_tick(tick_index, state_in):
        recv_big, recv_small, grad_enc_rows, grad_start_rows, sum_weights, sum_gains = state_in
        micro_index = tick_index - (sections - 1 - section_index)
        is_live = (micro_index >= 0) & (micro_index < MICRO)
        slot_index = jnp.clip(micro_index, 0, MICRO - 1)
        first_row = slot_index * per_micro
        big_in = kept_big[slot_index]
        small_in = kept_small[slot_index]
        length_part = lax.dynamic_slice_in_dim(lengths, first_row, per_micro, 0)
        cot_part = lax.dynamic_slice_in_dim(cotangent, first_row, per_micro, 0)
        grad_small_in = jnp.where(section_index == sections - 1, cot_part, recv_small)
        send_big, send_small, enc_grad, start_grad, term_stack, gain_stack = lax.switch(
            section_index,
            [backward_zero, backward_one, backward_two, backward_three],
            big_in,
            small_in,
            recv_big,
            grad_small_in,
            length_part,
            section_weights,
            gain_rows,
        )
        old_enc = lax.dynamic_slice_in_dim(grad_enc_rows, first_row, per_micro, 0)
        grad_enc_rows = lax.dynamic_update_slice_in_dim(
            grad_enc_rows, jnp.where(is_live, enc_grad, old_enc), first_row, 0
        )
        old_start = lax.dynamic_slice_in_dim(grad_start_rows, first_row, per_micro, 0)
        grad_start_rows = lax.dynamic_update_slice_in_dim(
            grad_start_rows, jnp.where(is_live, start_grad, old_start), first_row, 0
        )
        term_stack = jnp.where(is_live, term_stack, 0.0)
        gain_stack = jnp.where(is_live, gain_stack, 0.0)
        sum_weights = sum_weights + term_stack
        sum_gains = sum_gains + gain_stack
        recv_big, recv_small = (
            from_behind(shortened(send_big), "section", -1).astype(send_big.dtype),
            from_behind(shortened(send_small), "section", -1).astype(send_small.dtype),
        )
        return (recv_big, recv_small, grad_enc_rows, grad_start_rows, sum_weights, sum_gains)

    backward_state = lax.fori_loop(
        0,
        tick_count,
        backward_tick,
        (big_zero, small_zero, grad_enc_rows, grad_start_rows, sum_weights, sum_gains),
    )
    grad_enc_rows, grad_start_rows, sum_weights, sum_gains = (
        backward_state[2],
        backward_state[3],
        backward_state[4],
        backward_state[5],
    )
    decoded_full = decoded.astype(jnp.float32)
    enc_grad_out, decoded_out, start_grad_out = (
        lax.psum_scatter(
            grad_enc_rows.astype(jnp.bfloat16), "section", scatter_dimension=1, tiled=True
        ).astype(jnp.float32),
        lax.psum_scatter(
            decoded_full.astype(jnp.bfloat16), "section", scatter_dimension=1, tiled=True
        ).astype(jnp.float32),
        lax.psum_scatter(
            grad_start_rows.astype(jnp.bfloat16), "section", scatter_dimension=1, tiled=True
        ).astype(jnp.float32),
    )
    total_weights, total_gains = lax.psum((sum_weights, sum_gains), "dp")
    return (
        decoded_out.astype(jnp.bfloat16),
        enc_grad_out.astype(jnp.bfloat16),
        start_grad_out.astype(jnp.bfloat16),
        total_gains[None],
        total_weights[None],
    )


def solution(mesh):
    in_specs = (
        P("dp", "section", None),
        P("dp"),
        P("dp", "section"),
        P("section", None, None),
        P("section", None, None, None),
        P("dp", "section"),
    )
    out_specs = (
        P("dp", "section"),
        P("dp", "section", None),
        P("dp", "section"),
        P("section", None, None),
        P("section", None, None, None),
    )
    return jax.shard_map(local, mesh=mesh, in_specs=in_specs, out_specs=out_specs, check_vma=False)
```

profile of v0, /device:TPU:4, one launch (start us, length us, event | category | flops | bytes accessed | tf_op | source)
XLA Modules:
  0.0 1955.3 jit_solution(4872771433958979638)
XLA Ops:
  24.0 31.0 %all-gather.4.cloned.1.call-done = bf16[4,512,768]{2,1,0:T(8,128)(2,1)} async-done(((bf16[4,128,768]{2,1,0:T(8,128)(2,1)}), bf16[4,512,768]{2,1,0:T(8,128)(2,1)}) %all-gather.4.cloned.1.call-update) | async-done | bytes 3145744 | tf_op jit(solution)/shard_map/all_gather | solution.py:464
  57.1 291.7 %while.116 = (s32[]{:T(128)}, bf16[1,512,768]{2,1,0:T(8,128)(2,1)S(1)}, bf16[1,768]{1,0:T(2,128)(2,1)S(1)}, bf16[4,1,512,768]{3,2,1,0:T(8,128)(2,1)}, bf16[4,1,7...) while((s32[]{:T(128)}, ...), condition=%wide.region_18.19_spmd, body=%wide.region_0.18_spmd.sunk | while | flops 4850715648 | bytes 62178872 | solution.py:513
  81.4 18.2 collective-permute-done.3
  123.9 17.3 collective-permute-done.3
  165.5 16.4 collective-permute-done.3
  206.2 21.2 %collective-permute-done.3 = bf16[1,768]{1,0:T(2,128)(2,1)S(1)} collective-permute-done((bf16[1,768]{1,0:T(2,128)(2,1)S(1)}, bf16[1,768]{1,0:T(2,128)(2,1)S(1)}, u32[]{:S(2)}, u32[]{:S(2)}) %collective-permute-start.3) | collective-permute-done | bytes 1568 | tf_op jit(solution)/shard_map/while/body/eval_jaxpr/ppermute | solution.py:27
  327.0 21.8 %collective-permute-done.3 = bf16[1,768]{1,0:T(2,128)(2,1)S(1)} collective-permute-done((bf16[1,768]{1,0:T(2,128)(2,1)S(1)}, bf16[1,768]{1,0:T(2,128)(2,1)S(1)}, u32[]{:S(2)}, u32[]{:S(2)}) %collective-permute-start.3) | collective-permute-done | bytes 1568 | tf_op jit(solution)/shard_map/while/body/eval_jaxpr/ppermute | solution.py:27
  351.3 990.2 %while.117 = (s32[]{:T(128)}, bf16[1,512,768]{2,1,0:T(8,128)(2,1)S(1)}, bf16[1,768]{1,0:T(2,128)(2,1)S(1)}, bf16[4,512,768]{2,1,0:T(8,128)(2,1)}, bf16[4,768]{1,...) while((s32[]{:T(128)}, ...), condition=%wide.region_51.52_spmd.clone, body=%wide.region_20.51_spmd.clone.sunk | while | flops 12153526272 | bytes 254266704 | solution.py:562
  356.8 63.1 %conditional.6 = (bf16[1,512,768]{2,1,0:T(8,128)(2,1)}, bf16[1,768]{1,0:T(2,128)(2,1)S(1)}, bf16[1,512,768]{2,1,0:T(8,128)(2,1)S(1)}, bf16[1,768]{1,0:T(2,128)(2...) conditional(s32[]{:T(128)} %get-tuple-element.2279, ...), branch_computations={%region_21.35_spmd, %region_36.39_spmd, %region_40.47_spmd, %regio... | conditional | flops 12138971136 | bytes 188804752 | solution.py:533
  419.9 20.1 %collective-permute-start = (bf16[1,512,768]{2,1,0:T(8,128)(2,1)}, bf16[1,512,768]{2,1,0:T(8,128)(2,1)S(1)}, u32[]{:S(2)}, u32[]{:S(2)}) collective-permute-start(bf16[1,512,768]{2,1,0:T(8,128)(2,1)} %get-tuple-element.1846), channel_id=1, source_target_pairs={{8,0},{16,8},{24,16},{9,1},{17,9},{25,17},{10,2},{18,10},{26,18},{... | collective-permute-start | bytes 2359304 | tf_op jit(solution)/shard_map/while/body/eval_jaxpr/ppermute | solution.py:27
  440.1 45.3 %collective-permute-start.1 = (bf16[1,768]{1,0:T(2,128)(2,1)S(1)}, bf16[1,768]{1,0:T(2,128)(2,1)S(1)}, u32[]{:S(2)}, u32[]{:S(2)}) collective-permute-start(bf16[1,768]{1,0:T(2,128)(2,1)S(1)} %get-tuple-element.1847), channel_id=1, source_target_pairs={{8,0},{16,8},{24,16},{9,1},{17,9},{25,17},{10,2},{18,10},{26,18},{... | collective-permute-start | bytes 4616 | tf_op jit(solution)/shard_map/while/body/eval_jaxpr/ppermute | solution.py:27
  501.1 54.8 %conditional.6 = (bf16[1,512,768]{2,1,0:T(8,128)(2,1)}, bf16[1,768]{1,0:T(2,128)(2,1)S(1)}, bf16[1,512,768]{2,1,0:T(8,128)(2,1)S(1)}, bf16[1,768]{1,0:T(2,128)(2...) conditional(s32[]{:T(128)} %get-tuple-element.2279, ...), branch_computations={%region_21.35_spmd, %region_36.39_spmd, %region_40.47_spmd, %regio... | conditional | flops 12138971136 | bytes 188804752 | solution.py:533
  568.8 46.0 %collective-permute-start.1 = (bf16[1,768]{1,0:T(2,128)(2,1)S(1)}, bf16[1,768]{1,0:T(2,128)(2,1)S(1)}, u32[]{:S(2)}, u32[]{:S(2)}) collective-permute-start(bf16[1,768]{1,0:T(2,128)(2,1)S(1)} %get-tuple-element.1847), channel_id=1, source_target_pairs={{8,0},{16,8},{24,16},{9,1},{17,9},{25,17},{10,2},{18,10},{26,18},{... | collective-permute-start | bytes 4616 | tf_op jit(solution)/shard_map/while/body/eval_jaxpr/ppermute | solution.py:27
  614.9 18.7 select_add_fusion.4
  641.7 53.6 %conditional.6 = (bf16[1,512,768]{2,1,0:T(8,128)(2,1)}, bf16[1,768]{1,0:T(2,128)(2,1)S(1)}, bf16[1,512,768]{2,1,0:T(8,128)(2,1)S(1)}, bf16[1,768]{1,0:T(2,128)(2...) conditional(s32[]{:T(128)} %get-tuple-element.2279, ...), branch_computations={%region_21.35_spmd, %region_36.39_spmd, %region_40.47_spmd, %regio... | conditional | flops 12138971136 | bytes 188804752 | solution.py:533
  706.3 44.4 %collective-permute-start.1 = (bf16[1,768]{1,0:T(2,128)(2,1)S(1)}, bf16[1,768]{1,0:T(2,128)(2,1)S(1)}, u32[]{:S(2)}, u32[]{:S(2)}) collective-permute-start(bf16[1,768]{1,0:T(2,128)(2,1)S(1)} %get-tuple-element.1847), channel_id=1, source_target_pairs={{8,0},{16,8},{24,16},{9,1},{17,9},{25,17},{10,2},{18,10},{26,18},{... | collective-permute-start | bytes 4616 | tf_op jit(solution)/shard_map/while/body/eval_jaxpr/ppermute | solution.py:27
  750.8 18.7 select_add_fusion.4
  777.6 53.6 %conditional.6 = (bf16[1,512,768]{2,1,0:T(8,128)(2,1)}, bf16[1,768]{1,0:T(2,128)(2,1)S(1)}, bf16[1,512,768]{2,1,0:T(8,128)(2,1)S(1)}, bf16[1,768]{1,0:T(2,128)(2...) conditional(s32[]{:T(128)} %get-tuple-element.2279, ...), branch_computations={%region_21.35_spmd, %region_36.39_spmd, %region_40.47_spmd, %regio... | conditional | flops 12138971136 | bytes 188804752 | solution.py:533
  845.5 40.5 %collective-permute-start.1 = (bf16[1,768]{1,0:T(2,128)(2,1)S(1)}, bf16[1,768]{1,0:T(2,128)(2,1)S(1)}, u32[]{:S(2)}, u32[]{:S(2)}) collective-permute-start(bf16[1,768]{1,0:T(2,128)(2,1)S(1)} %get-tuple-element.1847), channel_id=1, source_target_pairs={{8,0},{16,8},{24,16},{9,1},{17,9},{25,17},{10,2},{18,10},{26,18},{... | collective-permute-start | bytes 4616 | tf_op jit(solution)/shard_map/while/body/eval_jaxpr/ppermute | solution.py:27
  886.1 18.7 select_add_fusion.4
  912.9 53.6 %conditional.6 = (bf16[1,512,768]{2,1,0:T(8,128)(2,1)}, bf16[1,768]{1,0:T(2,128)(2,1)S(1)}, bf16[1,512,768]{2,1,0:T(8,128)(2,1)S(1)}, bf16[1,768]{1,0:T(2,128)(2...) conditional(s32[]{:T(128)} %get-tuple-element.2279, ...), branch_computations={%region_21.35_spmd, %region_36.39_spmd, %region_40.47_spmd, %regio... | conditional | flops 12138971136 | bytes 188804752 | solution.py:533
  981.0 62.1 %collective-permute-start.1 = (bf16[1,768]{1,0:T(2,128)(2,1)S(1)}, bf16[1,768]{1,0:T(2,128)(2,1)S(1)}, u32[]{:S(2)}, u32[]{:S(2)}) collective-permute-start(bf16[1,768]{1,0:T(2,128)(2,1)S(1)} %get-tuple-element.1847), channel_id=1, source_target_pairs={{8,0},{16,8},{24,16},{9,1},{17,9},{25,17},{10,2},{18,10},{26,18},{... | collective-permute-start | bytes 4616 | tf_op jit(solution)/shard_map/while/body/eval_jaxpr/ppermute | solution.py:27
  1043.2 18.7 select_add_fusion.4
  1070.0 53.6 %conditional.6 = (bf16[1,512,768]{2,1,0:T(8,128)(2,1)}, bf16[1,768]{1,0:T(2,128)(2,1)S(1)}, bf16[1,512,768]{2,1,0:T(8,128)(2,1)S(1)}, bf16[1,768]{1,0:T(2,128)(2...) conditional(s32[]{:T(128)} %get-tuple-element.2279, ...), branch_computations={%region_21.35_spmd, %region_36.39_spmd, %region_40.47_spmd, %regio... | conditional | flops 12138971136 | bytes 188804752 | solution.py:533
  1138.5 62.0 %collective-permute-start.1 = (bf16[1,768]{1,0:T(2,128)(2,1)S(1)}, bf16[1,768]{1,0:T(2,128)(2,1)S(1)}, u32[]{:S(2)}, u32[]{:S(2)}) collective-permute-start(bf16[1,768]{1,0:T(2,128)(2,1)S(1)} %get-tuple-element.1847), channel_id=1, source_target_pairs={{8,0},{16,8},{24,16},{9,1},{17,9},{25,17},{10,2},{18,10},{26,18},{... | collective-permute-start | bytes 4616 | tf_op jit(solution)/shard_map/while/body/eval_jaxpr/ppermute | solution.py:27
  1223.4 53.6 %conditional.6 = (bf16[1,512,768]{2,1,0:T(8,128)(2,1)}, bf16[1,768]{1,0:T(2,128)(2,1)S(1)}, bf16[1,512,768]{2,1,0:T(8,128)(2,1)S(1)}, bf16[1,768]{1,0:T(2,128)(2...) conditional(s32[]{:T(128)} %get-tuple-element.2279, ...), branch_computations={%region_21.35_spmd, %region_36.39_spmd, %region_40.47_spmd, %regio... | conditional | flops 12138971136 | bytes 188804752 | solution.py:533
  1277.0 18.3 collective-permute-start
  1295.3 26.9 %collective-permute-start.1 = (bf16[1,768]{1,0:T(2,128)(2,1)S(1)}, bf16[1,768]{1,0:T(2,128)(2,1)S(1)}, u32[]{:S(2)}, u32[]{:S(2)}) collective-permute-start(bf16[1,768]{1,0:T(2,128)(2,1)S(1)} %get-tuple-element.1847), channel_id=1, source_target_pairs={{8,0},{16,8},{24,16},{9,1},{17,9},{25,17},{10,2},{18,10},{26,18},{... | collective-permute-start | bytes 4616 | tf_op jit(solution)/shard_map/while/body/eval_jaxpr/ppermute | solution.py:27
  1346.0 133.5 %psum.14 = f32[1,2,768]{2,1,0:T(2,128)} all-reduce(f32[1,2,768]{2,1,0:T(2,128)S(1)} %bitcast.740), channel_id=1, replica_groups=mesh['section'=4,'dp'=8] {'dp'}, use_global_device_ids=true, to_apply=%region_54.55 | all-reduce | flops 1536 | bytes 12288 | tf_op jit(solution)/shard_map/psum | solution.py:586
  1487.6 25.3 %reduce-scatter.10.cloned.1.call-done = bf16[192,4]{1,0:T(8,128)(2,1)} async-done(((bf16[768,4]{1,0:T(8,128)(2,1)}), bf16[192,4]{1,0:T(8,128)(2,1)}) %reduce-scatter.10.cloned.1.call-update) | async-done | bytes 1552
  1514.4 45.9 %reduce-scatter.8.cloned.1.call-done = bf16[4,128,768]{2,1,0:T(8,128)(2,1)} async-done(((bf16[4,512,768]{2,1,0:T(8,128)(2,1)}), bf16[4,128,768]{2,1,0:T(8,128)(2,1)}) %reduce-scatter.8.cloned.1.call-update) | async-done | bytes 786448 | tf_op jit(solution)/shard_map/reduce_scatter | solution.py:576
  1560.2 375.2 %all-reduce.5.cloned.1.call-done = f32[1,8,768,768]{3,2,1,0:T(8,128)} async-done(((f32[1,8,768,768]{3,2,1,0:T(8,128)}), f32[1,8,768,768]{3,2,1,0:T(8,128)}) %all-reduce.5.cloned.1.call-update) | async-done | bytes 18874384 | tf_op jit(solution)/shard_map/psum | solution.py:586
  (980 shorter events, 853.8 us)
Async XLA Ops:
  7.2 47.9 %all-gather.4.cloned.1.call-start = ((), (), s32[]{:S(2)}) async-start(), calls=%async_computation.3 | async-start | bytes 3932160 | tf_op jit(solution)/shard_map/all_gather | solution.py:464
  7.9 1478.2 %reduce-scatter.12.cloned.1.call-start = ((), (), s32[]{:S(2)}) async-start(), calls=%async_computation.7 | async-start | bytes 245760
  77.5 22.1 %collective-permute-start.2 = (bf16[1,512,768]{2,1,0:T(8,128)(2,1)S(1)}, bf16[1,512,768]{2,1,0:T(8,128)(2,1)S(1)}, u32[]{:S(2)}, u32[]{:S(2)}) collective-permute-start(bf16[1,512,768]{2,1,0:T(8,128)(2,1)S(1)} %get-tuple-element.1826), channel_id=1, source_target_pairs={{0,8},{8,16},{16,24},{1,9},{9,17},{17,25},{2,10},{10,18},{18,26},{... | collective-permute-start | bytes 2359304 | tf_op jit(solution)/shard_map/while/body/eval_jaxpr/ppermute | solution.py:27
  79.4 20.2 %collective-permute-start.3 = (bf16[1,768]{1,0:T(2,128)(2,1)S(1)}, bf16[1,768]{1,0:T(2,128)(2,1)S(1)}, u32[]{:S(2)}, u32[]{:S(2)}) collective-permute-start(bf16[1,768]{1,0:T(2,128)(2,1)S(1)} %get-tuple-element.1827), channel_id=1, source_target_pairs={{0,8},{8,16},{16,24},{1,9},{9,17},{17,25},{2,10},{10,18},{18,26},{... | collective-permute-start | bytes 4616 | tf_op jit(solution)/shard_map/while/body/eval_jaxpr/ppermute | solution.py:27
  120.0 21.3 %collective-permute-start.2 = (bf16[1,512,768]{2,1,0:T(8,128)(2,1)S(1)}, bf16[1,512,768]{2,1,0:T(8,128)(2,1)S(1)}, u32[]{:S(2)}, u32[]{:S(2)}) collective-permute-start(bf16[1,512,768]{2,1,0:T(8,128)(2,1)S(1)} %get-tuple-element.1826), channel_id=1, source_target_pairs={{0,8},{8,16},{16,24},{1,9},{9,17},{17,25},{2,10},{10,18},{18,26},{... | collective-permute-start | bytes 2359304 | tf_op jit(solution)/shard_map/while/body/eval_jaxpr/ppermute | solution.py:27
  121.9 19.3 collective-permute-start.3
  161.6 20.3 %collective-permute-start.2 = (bf16[1,512,768]{2,1,0:T(8,128)(2,1)S(1)}, bf16[1,512,768]{2,1,0:T(8,128)(2,1)S(1)}, u32[]{:S(2)}, u32[]{:S(2)}) collective-permute-start(bf16[1,512,768]{2,1,0:T(8,128)(2,1)S(1)} %get-tuple-element.1826), channel_id=1, source_target_pairs={{0,8},{8,16},{16,24},{1,9},{9,17},{17,25},{2,10},{10,18},{18,26},{... | collective-permute-start | bytes 2359304 | tf_op jit(solution)/shard_map/while/body/eval_jaxpr/ppermute | solution.py:27
  163.5 18.4 collective-permute-start.3
  202.3 25.2 %collective-permute-start.2 = (bf16[1,512,768]{2,1,0:T(8,128)(2,1)S(1)}, bf16[1,512,768]{2,1,0:T(8,128)(2,1)S(1)}, u32[]{:S(2)}, u32[]{:S(2)}) collective-permute-start(bf16[1,512,768]{2,1,0:T(8,128)(2,1)S(1)} %get-tuple-element.1826), channel_id=1, source_target_pairs={{0,8},{8,16},{16,24},{1,9},{9,17},{17,25},{2,10},{10,18},{18,26},{... | collective-permute-start | bytes 2359304 | tf_op jit(solution)/shard_map/while/body/eval_jaxpr/ppermute | solution.py:27
  204.2 23.2 %collective-permute-start.3 = (bf16[1,768]{1,0:T(2,128)(2,1)S(1)}, bf16[1,768]{1,0:T(2,128)(2,1)S(1)}, u32[]{:S(2)}, u32[]{:S(2)}) collective-permute-start(bf16[1,768]{1,0:T(2,128)(2,1)S(1)} %get-tuple-element.1827), channel_id=1, source_target_pairs={{0,8},{8,16},{16,24},{1,9},{9,17},{17,25},{2,10},{10,18},{18,26},{... | collective-permute-start | bytes 4616 | tf_op jit(solution)/shard_map/while/body/eval_jaxpr/ppermute | solution.py:27
  247.7 17.2 collective-permute-start.2
  285.3 17.4 collective-permute-start.2
  287.2 15.5 collective-permute-start.3
  323.1 25.8 %collective-permute-start.2 = (bf16[1,512,768]{2,1,0:T(8,128)(2,1)S(1)}, bf16[1,512,768]{2,1,0:T(8,128)(2,1)S(1)}, u32[]{:S(2)}, u32[]{:S(2)}) collective-permute-start(bf16[1,512,768]{2,1,0:T(8,128)(2,1)S(1)} %get-tuple-element.1826), channel_id=1, source_target_pairs={{0,8},{8,16},{16,24},{1,9},{9,17},{17,25},{2,10},{10,18},{18,26},{... | collective-permute-start | bytes 2359304 | tf_op jit(solution)/shard_map/while/body/eval_jaxpr/ppermute | solution.py:27
  325.0 23.8 %collective-permute-start.3 = (bf16[1,768]{1,0:T(2,128)(2,1)S(1)}, bf16[1,768]{1,0:T(2,128)(2,1)S(1)}, u32[]{:S(2)}, u32[]{:S(2)}) collective-permute-start(bf16[1,768]{1,0:T(2,128)(2,1)S(1)} %get-tuple-element.1827), channel_id=1, source_target_pairs={{0,8},{8,16},{16,24},{1,9},{9,17},{17,25},{2,10},{10,18},{18,26},{... | collective-permute-start | bytes 4616 | tf_op jit(solution)/shard_map/while/body/eval_jaxpr/ppermute | solution.py:27
  419.9 75.0 %collective-permute-start = (bf16[1,512,768]{2,1,0:T(8,128)(2,1)}, bf16[1,512,768]{2,1,0:T(8,128)(2,1)S(1)}, u32[]{:S(2)}, u32[]{:S(2)}) collective-permute-start(bf16[1,512,768]{2,1,0:T(8,128)(2,1)} %get-tuple-element.1846), channel_id=1, source_target_pairs={{8,0},{16,8},{24,16},{9,1},{17,9},{25,17},{10,2},{18,10},{26,18},{... | collective-permute-start | bytes 2359304 | tf_op jit(solution)/shard_map/while/body/eval_jaxpr/ppermute | solution.py:27
  440.1 54.9 %collective-permute-start.1 = (bf16[1,768]{1,0:T(2,128)(2,1)S(1)}, bf16[1,768]{1,0:T(2,128)(2,1)S(1)}, u32[]{:S(2)}, u32[]{:S(2)}) collective-permute-start(bf16[1,768]{1,0:T(2,128)(2,1)S(1)} %get-tuple-element.1847), channel_id=1, source_target_pairs={{8,0},{16,8},{24,16},{9,1},{17,9},{25,17},{10,2},{18,10},{26,18},{... | collective-permute-start | bytes 4616 | tf_op jit(solution)/shard_map/while/body/eval_jaxpr/ppermute | solution.py:27
  555.8 80.1 %collective-permute-start = (bf16[1,512,768]{2,1,0:T(8,128)(2,1)}, bf16[1,512,768]{2,1,0:T(8,128)(2,1)S(1)}, u32[]{:S(2)}, u32[]{:S(2)}) collective-permute-start(bf16[1,512,768]{2,1,0:T(8,128)(2,1)} %get-tuple-element.1846), channel_id=1, source_target_pairs={{8,0},{16,8},{24,16},{9,1},{17,9},{25,17},{10,2},{18,10},{26,18},{... | collective-permute-start | bytes 2359304 | tf_op jit(solution)/shard_map/while/body/eval_jaxpr/ppermute | solution.py:27
  568.8 67.0 %collective-permute-start.1 = (bf16[1,768]{1,0:T(2,128)(2,1)S(1)}, bf16[1,768]{1,0:T(2,128)(2,1)S(1)}, u32[]{:S(2)}, u32[]{:S(2)}) collective-permute-start(bf16[1,768]{1,0:T(2,128)(2,1)S(1)} %get-tuple-element.1847), channel_id=1, source_target_pairs={{8,0},{16,8},{24,16},{9,1},{17,9},{25,17},{10,2},{18,10},{26,18},{... | collective-permute-start | bytes 4616 | tf_op jit(solution)/shard_map/while/body/eval_jaxpr/ppermute | solution.py:27
  695.3 76.4 %collective-permute-start = (bf16[1,512,768]{2,1,0:T(8,128)(2,1)}, bf16[1,512,768]{2,1,0:T(8,128)(2,1)S(1)}, u32[]{:S(2)}, u32[]{:S(2)}) collective-permute-start(bf16[1,512,768]{2,1,0:T(8,128)(2,1)} %get-tuple-element.1846), channel_id=1, source_target_pairs={{8,0},{16,8},{24,16},{9,1},{17,9},{25,17},{10,2},{18,10},{26,18},{... | collective-permute-start | bytes 2359304 | tf_op jit(solution)/shard_map/while/body/eval_jaxpr/ppermute | solution.py:27
  706.3 65.5 %collective-permute-start.1 = (bf16[1,768]{1,0:T(2,128)(2,1)S(1)}, bf16[1,768]{1,0:T(2,128)(2,1)S(1)}, u32[]{:S(2)}, u32[]{:S(2)}) collective-permute-start(bf16[1,768]{1,0:T(2,128)(2,1)S(1)} %get-tuple-element.1847), channel_id=1, source_target_pairs={{8,0},{16,8},{24,16},{9,1},{17,9},{25,17},{10,2},{18,10},{26,18},{... | collective-permute-start | bytes 4616 | tf_op jit(solution)/shard_map/while/body/eval_jaxpr/ppermute | solution.py:27
  831.2 75.9 %collective-permute-start = (bf16[1,512,768]{2,1,0:T(8,128)(2,1)}, bf16[1,512,768]{2,1,0:T(8,128)(2,1)S(1)}, u32[]{:S(2)}, u32[]{:S(2)}) collective-permute-start(bf16[1,512,768]{2,1,0:T(8,128)(2,1)} %get-tuple-element.1846), channel_id=1, source_target_pairs={{8,0},{16,8},{24,16},{9,1},{17,9},{25,17},{10,2},{18,10},{26,18},{... | collective-permute-start | bytes 2359304 | tf_op jit(solution)/shard_map/while/body/eval_jaxpr/ppermute | solution.py:27
  845.5 61.5 %collective-permute-start.1 = (bf16[1,768]{1,0:T(2,128)(2,1)S(1)}, bf16[1,768]{1,0:T(2,128)(2,1)S(1)}, u32[]{:S(2)}, u32[]{:S(2)}) collective-permute-start(bf16[1,768]{1,0:T(2,128)(2,1)S(1)} %get-tuple-element.1847), channel_id=1, source_target_pairs={{8,0},{16,8},{24,16},{9,1},{17,9},{25,17},{10,2},{18,10},{26,18},{... | collective-permute-start | bytes 4616 | tf_op jit(solution)/shard_map/while/body/eval_jaxpr/ppermute | solution.py:27
  966.5 97.7 %collective-permute-start = (bf16[1,512,768]{2,1,0:T(8,128)(2,1)}, bf16[1,512,768]{2,1,0:T(8,128)(2,1)S(1)}, u32[]{:S(2)}, u32[]{:S(2)}) collective-permute-start(bf16[1,512,768]{2,1,0:T(8,128)(2,1)} %get-tuple-element.1846), channel_id=1, source_target_pairs={{8,0},{16,8},{24,16},{9,1},{17,9},{25,17},{10,2},{18,10},{26,18},{... | collective-permute-start | bytes 2359304 | tf_op jit(solution)/shard_map/while/body/eval_jaxpr/ppermute | solution.py:27
  981.0 83.2 %collective-permute-start.1 = (bf16[1,768]{1,0:T(2,128)(2,1)S(1)}, bf16[1,768]{1,0:T(2,128)(2,1)S(1)}, u32[]{:S(2)}, u32[]{:S(2)}) collective-permute-start(bf16[1,768]{1,0:T(2,128)(2,1)S(1)} %get-tuple-element.1847), channel_id=1, source_target_pairs={{8,0},{16,8},{24,16},{9,1},{17,9},{25,17},{10,2},{18,10},{26,18},{... | collective-permute-start | bytes 4616 | tf_op jit(solution)/shard_map/while/body/eval_jaxpr/ppermute | solution.py:27
  1123.6 93.9 %collective-permute-start = (bf16[1,512,768]{2,1,0:T(8,128)(2,1)}, bf16[1,512,768]{2,1,0:T(8,128)(2,1)S(1)}, u32[]{:S(2)}, u32[]{:S(2)}) collective-permute-start(bf16[1,512,768]{2,1,0:T(8,128)(2,1)} %get-tuple-element.1846), channel_id=1, source_target_pairs={{8,0},{16,8},{24,16},{9,1},{17,9},{25,17},{10,2},{18,10},{26,18},{... | collective-permute-start | bytes 2359304 | tf_op jit(solution)/shard_map/while/body/eval_jaxpr/ppermute | solution.py:27
  1138.5 79.1 %collective-permute-start.1 = (bf16[1,768]{1,0:T(2,128)(2,1)S(1)}, bf16[1,768]{1,0:T(2,128)(2,1)S(1)}, u32[]{:S(2)}, u32[]{:S(2)}) collective-permute-start(bf16[1,768]{1,0:T(2,128)(2,1)S(1)} %get-tuple-element.1847), channel_id=1, source_target_pairs={{8,0},{16,8},{24,16},{9,1},{17,9},{25,17},{10,2},{18,10},{26,18},{... | collective-permute-start | bytes 4616 | tf_op jit(solution)/shard_map/while/body/eval_jaxpr/ppermute | solution.py:27
  1277.0 62.4 %collective-permute-start = (bf16[1,512,768]{2,1,0:T(8,128)(2,1)}, bf16[1,512,768]{2,1,0:T(8,128)(2,1)S(1)}, u32[]{:S(2)}, u32[]{:S(2)}) collective-permute-start(bf16[1,512,768]{2,1,0:T(8,128)(2,1)} %get-tuple-element.1846), channel_id=1, source_target_pairs={{8,0},{16,8},{24,16},{9,1},{17,9},{25,17},{10,2},{18,10},{26,18},{... | collective-permute-start | bytes 2359304 | tf_op jit(solution)/shard_map/while/body/eval_jaxpr/ppermute | solution.py:27
  1295.3 44.0 %collective-permute-start.1 = (bf16[1,768]{1,0:T(2,128)(2,1)S(1)}, bf16[1,768]{1,0:T(2,128)(2,1)S(1)}, u32[]{:S(2)}, u32[]{:S(2)}) collective-permute-start(bf16[1,768]{1,0:T(2,128)(2,1)S(1)} %get-tuple-element.1847), channel_id=1, source_target_pairs={{8,0},{16,8},{24,16},{9,1},{17,9},{25,17},{10,2},{18,10},{26,18},{... | collective-permute-start | bytes 4616 | tf_op jit(solution)/shard_map/while/body/eval_jaxpr/ppermute | solution.py:27
  1343.1 169.8 %reduce-scatter.10.cloned.1.call-start = ((), (), s32[]{:S(2)}) async-start(), calls=%async_computation.6 | async-start | bytes 245760
  1344.7 215.5 %reduce-scatter.8.cloned.1.call-start = ((), (), s32[]{:S(2)}) async-start(), calls=%async_computation.4 | async-start | bytes 3932160 | tf_op jit(solution)/shard_map/reduce_scatter | solution.py:576
  1345.3 590.2 %all-reduce.5.cloned.1.call-start = ((), (), s32[]{:S(2)}) async-start(), calls=%async_computation.5 | async-start | bytes 37748736 | tf_op jit(solution)/shard_map/psum | solution.py:586
  (95 other events, 713.5 us)
Sparse Core Ops, SparseCore 0:
  9.9 45.1 all-gather.3
  1343.2 142.8 reduce-scatter.11
  1488.9 23.9 reduce-scatter.9
  1516.3 43.8 reduce-scatter.7
  1563.2 372.2 all-reduce.4
where the time goes:
time: 1980 us; the launch traced here: 1960 us
  waiting for transfers between devices  608 us (31%)
  starting transfers between devices  460 us (23%)
  matrix products  271 us (14%)
  other arithmetic  232 us (12%)
  local copies, waits for them, and re-layouts  172 us (9%)
  blocking collectives  149 us (8%)
  loops' own time  48.9 us (2%)
    ppermute x28, starting transfers between devices, from_behind(): return lax.ppermute(block, axis, route)  460 us
    psum x1, waiting for transfers between devices, local(): total_weights, total_gains = lax.psum((sum_weights, sum_gains), 'dp')  375 us
    dot_general x77, matrix products, product(): result = jnp.dot(flattened, right_side, preferred_element_type=jnp.float32)  142 us
    psum x1, blocking collectives, local(): total_weights, total_gains = lax.psum((sum_weights, sum_gains), 'dp')  133 us
    ppermute x28, waiting for transfers between devices, from_behind(): return lax.ppermute(block, axis, route)  122 us
    add x7, other arithmetic, backward_tick(): sum_weights = sum_weights + term_stack  111 us
    dot_general x42, matrix products, product_back(): lax.dot_general(flattened, right_side, (((1,), (1,)), ((), ())), preferre...  86.6 us
    cond x28, other arithmetic  46.6 us
  transfers between devices with their start and end apart: 33, of which 12 were waited for; matrix products, arithmetic and copies ran while one was open for 7% of the time, Pallas kernels for 0%

commit v1 on v0

v1 whole, which is shorter than its diff:
```python
import functools
import math

import jax
import jax.numpy as jnp
from jax import lax
from jax.experimental import pallas as pl
from jax.experimental.pallas import tpu as pltpu
from jax.sharding import PartitionSpec as P

D = 768
HEADS = 12
HEAD = 64
PAIRS = HEADS // 2
LEN = 512
GROUP = 4
ROWS = GROUP * LEN
epsilon = 1e-06
masked_score = -1e30
gelu_coeff = 0.044715
gelu_scale = math.sqrt(2.0 / math.pi)
log2_e = 1.4426950408889634
bf16 = jnp.bfloat16
f32 = jnp.float32
MESH = pl.DeviceIdType.MESH

W_ROWS = 0
X_ROWS = 3072
Q_ROWS = X_ROWS + ROWS
K_ROWS = Q_ROWS + ROWS
V_ROWS = K_ROWS + ROWS
O_ROWS = V_ROWS + ROWS
H_ROWS = O_ROWS + ROWS
DH_ROWS = H_ROWS + ROWS
IL_ROWS = DH_ROWS + ROWS
POOL_ROWS = IL_ROWS + ROWS
FF_H = 6144
FF_A = FF_H + ROWS
FF_E = FF_A + ROWS
RELAY_F = 6144
GELU_ROWS = 12 * ROWS
WIDE_ROWS = 24 * ROWS

CHUNK = 64
CHUNKS = 4
RELAY = CHUNK * CHUNKS
DIRECT = LEN - RELAY
RELAY_B = RELAY_F + GROUP * RELAY
FAC_ROWS = 176


def nn(a, b):
    return jnp.dot(a, b, preferred_element_type=f32)


def nt(a, b):
    return lax.dot_general(a, b, (((1,), (1,)), ((), ())), preferred_element_type=f32)


def tn(a, b):
    return lax.dot_general(a, b, (((0,), (0,)), ((), ())), preferred_element_type=f32)


def iota(shape, axis):
    return lax.broadcasted_iota(jnp.int32, shape, axis)


def inverse_rms(v):
    return lax.rsqrt(jnp.mean(v * v, axis=-1, keepdims=True) + epsilon)


def norm_back(normed, inverse, gain_row, grad):
    scaled = grad * gain_row
    return inverse * (scaled - normed * jnp.mean(scaled * normed, axis=-1, keepdims=True))


def gelu_both(u):
    square = u * u
    tangent = jnp.tanh(gelu_scale * (u + gelu_coeff * square * u))
    half = 0.5 * (1.0 + tangent)
    slope = half + 0.5 * u * (1.0 - tangent * tangent) * (
        gelu_scale + 3.0 * gelu_coeff * gelu_scale * square
    )
    return (u * half, slope)


class Places:
    def __init__(self, sections):
        self.count = 0
        self.enc = [self.take(GROUP) for _ in range(sections)]
        self.small = [self.take(2) for _ in range(sections)]
        self.direct = self.take(GROUP)
        self.relay = [self.take(GROUP * CHUNKS) for _ in range(3)]
        self.back_direct = self.take(GROUP)
        self.back_relay = [self.take(GROUP * CHUNKS) for _ in range(3)]
        self.qk = self.take(1)
        self.mix = self.take(GROUP)
        self.state = self.take(1)
        self.state_back = self.take(1)
        self.g = self.take(1)
        self.x = self.take(1)
        self.out_enc = [self.take(GROUP) for _ in range(sections)]
        self.out_small = [self.take(2) for _ in range(sections)]

    def take(self, amount):
        first = self.count
        self.count += amount
        return first


def relay_kernel(
    sections,
    places,
    len_ref,
    enc_ref,
    small_ref,
    w_ref,
    gain_ref,
    o_enc,
    o_small,
    o_dw,
    o_fac,
    o_gain,
    pool,
    wide,
    acc,
    cp,
    small,
    qk,
    mix,
    gk,
    xs,
    state,
    state_back,
    fac,
    rows_out,
    gain_sum,
    send_sem,
    recv_sem,
    local_sem,
):
    me = lax.axis_index("section")
    group = lax.axis_index("dp")
    chunk_len = LEN // sections

    def remote(number, src, dst, target):
        return pltpu.make_async_remote_copy(
            src_ref=src,
            dst_ref=dst,
            send_sem=send_sem.at[number],
            recv_sem=recv_sem.at[number],
            device_id=(target, group),
            device_id_type=MESH,
        )

    def local_copy(number, src, dst):
        return pltpu.make_async_copy(src, dst, local_sem.at[number])

    def rows(base, start, count):
        return pool.at[pl.ds(pl.multiple_of(base + start, CHUNK), count)]

    barrier = pltpu.get_barrier_semaphore()
    for step in range(1, sections):
        pl.semaphore_signal(
            barrier,
            inc=1,
            device_id=(lax.rem(me + step, sections), group),
            device_id_type=MESH,
        )
    pl.semaphore_wait(barrier, sections - 1)

    lane = iota((1, 128), 1)
    low_half = lane < HEAD

    def enc_copy(sender, p):
        return remote(
            places.enc[sender] + p,
            enc_ref.at[p],
            rows(X_ROWS, p * LEN + sender * chunk_len, chunk_len),
            0,
        )

    def small_copy(sender, target):
        return remote(places.small[sender] + target - 2, small_ref, small.at[sender], target)

    def direct_copy(p):
        return remote(
            places.direct + p, rows(H_ROWS, p * LEN, DIRECT), rows(FF_H, p * LEN, DIRECT), 1
        )

    def relay_copy(hop, index):
        p = index // CHUNKS
        piece = index % CHUNKS
        whole = p * LEN + DIRECT + piece * CHUNK
        src = rows(H_ROWS, whole, CHUNK) if hop == 0 else rows(RELAY_F, index * CHUNK, CHUNK)
        dst = rows(FF_H, whole, CHUNK) if hop == 2 else rows(RELAY_F, index * CHUNK, CHUNK)
        return remote(places.relay[hop] + index, src, dst, (2, 3, 1)[hop])

    def back_direct_copy(p):
        return remote(
            places.back_direct + p, rows(FF_H, p * LEN, DIRECT), rows(DH_ROWS, p * LEN, DIRECT), 0
        )

    def back_relay_copy(hop, index):
        p = index // CHUNKS
        piece = index % CHUNKS
        whole = p * LEN + DIRECT + piece * CHUNK
        src = rows(FF_H, whole, CHUNK) if hop == 0 else rows(RELAY_B, index * CHUNK, CHUNK)
        dst = rows(DH_ROWS, whole, CHUNK) if hop == 2 else rows(RELAY_B, index * CHUNK, CHUNK)
        return remote(places.back_relay[hop] + index, src, dst, (3, 2, 0)[hop])

    def qk_copy():
        return remote(places.qk, qk, qk, 1)

    def mix_copy(p):
        part = pl.ds(pl.multiple_of(p * 16, 16), 16)
        return remote(places.mix + p, mix.at[part], mix.at[part], 2)

    def state_copy():
        return remote(places.state, state, state, 3)

    def state_back_copy():
        return remote(places.state_back, state_back, state_back, 2)

    def g_copy():
        return remote(places.g, gk, gk, 1)

    def x_copy():
        return remote(places.x, xs, xs, 2)

    def out_enc_copy(target, p):
        return remote(
            places.out_enc[target] + p,
            rows(H_ROWS, p * LEN + target * chunk_len, chunk_len),
            o_enc.at[p],
            target,
        )

    def out_small_copy(target, kind):
        return remote(
            places.out_small[target] + kind, rows_out.at[kind], o_small.at[kind], target
        )

    def each_passage(body):
        def step(p, carry):
            body(p)
            return carry

        lax.fori_loop(0, GROUP, step, 0)

    def weights_in(blocks):
        copies = [
            local_copy(
                i,
                w_ref.at[pl.ds(i * D, D)],
                pool.at[pl.ds(W_ROWS + i * D, D)],
            )
            for i in range(blocks)
        ]
        for c in copies:
            c.start()
        return copies

    def block(i):
        return pool[W_ROWS + i * D : W_ROWS + (i + 1) * D, :]

    def send_inputs():
        def step(p, carry):
            enc_copy(me, p).start()
            return carry

        lax.fori_loop(0, GROUP, step, 0)

    def dynamic_enc_copy(p):
        number = places.enc[0] + me * GROUP + p
        return remote(
            number, enc_ref.at[p], rows(X_ROWS, p * LEN + me * chunk_len, chunk_len), 0
        )

    def dynamic_small_copy(target):
        number = places.small[0] + me * 2 + target - 2
        return remote(number, small_ref, small.at[me], target)

    @pl.when(me != 2)
    def _():
        dynamic_small_copy(2).start()

    @pl.when(me != 3)
    def _():
        dynamic_small_copy(3).start()

    @pl.when(me != 0)
    def _():
        each_passage(lambda p: dynamic_enc_copy(p).start())

    @pl.when(me == 0)
    def _():
        own = [
            local_copy(8 + p, enc_ref.at[p], pool.at[pl.ds(X_ROWS + p * LEN, chunk_len)])
            for p in range(GROUP)
        ]
        for c in own:
            c.start()
        weights = weights_in(4)
        for c in weights:
            c.wait()
        for c in own:
            c.wait()
        gain_row = gain_ref[0:1, :]
        key_row = iota((LEN, 1), 0)

        def pair_columns(hp):
            return pl.ds(pl.multiple_of(hp * 128, 128), 128)

        def forward(p):
            for sender in range(1, sections):
                enc_copy(sender, p).wait_recv()
            start = pl.multiple_of(p * LEN, LEN)
            x = pool[pl.ds(X_ROWS + start, LEN), :].astype(f32)
            a0 = (x * inverse_rms(x) * gain_row).astype(bf16)
            pool[pl.ds(Q_ROWS + start, LEN), :] = (nn(a0, block(0)) * log2_e).astype(bf16)
            pool[pl.ds(K_ROWS + start, LEN), :] = nn(a0, block(1)).astype(bf16)
            pool[pl.ds(V_ROWS + start, LEN), :] = nn(a0, block(2)).astype(bf16)
            bias = jnp.where(key_row < len_ref[p], 0.0, masked_score).astype(bf16)

            def pair(hp, carry):
                c = pair_columns(hp)
                q2 = pool[pl.ds(Q_ROWS + start, LEN), c]
                k2 = pool[pl.ds(K_ROWS + start, LEN), c]
                v2 = pool[pl.ds(V_ROWS + start, LEN), c]
                one = jnp.ones_like(q2)
                zero = jnp.zeros_like(q2)
                queries = [
                    jnp.where(low_half, q2, jnp.where(lane == HEAD, one, zero)),
                    jnp.where(low_half, jnp.where(lane == 0, one, zero), q2),
                ]
                keys = [
                    jnp.where(low_half, k2, jnp.where(lane == HEAD, bias, zero)),
                    jnp.where(low_half, jnp.where(lane == 0, bias, zero), k2),
                ]
                values = [jnp.where(low_half, v2, one), jnp.where(low_half, one, v2)]
                mixes = []
                for half in range(2):
                    s = nt(queries[half], keys[half])
                    e = jnp.exp2(s - jnp.max(s, axis=-1, keepdims=True)).astype(bf16)
                    at = pl.multiple_of((p * HEADS + hp * 2 + half) * 2 * LEN, 2 * LEN)
                    wide[pl.ds(at, LEN), :] = e[:, :256]
                    wide[pl.ds(at + LEN, LEN), :] = e[:, 256:]
                    mixes.append(nn(e, values[half]))
                total = pltpu.roll(jnp.where(low_half, mixes[1], mixes[0]), HEAD, 1)
                inverse = 1.0 / total
                pool[pl.ds(O_ROWS + start, LEN), c] = (
                    jnp.where(low_half, mixes[0], mixes[1]) * inverse
                ).astype(bf16)
                pool[pl.ds(IL_ROWS + start, LEN), c] = inverse.astype(bf16)
                return carry

            lax.fori_loop(0, PAIRS, pair, 0)
            h = x + nn(pool[pl.ds(O_ROWS + start, LEN), :], block(3))
            pool[pl.ds(H_ROWS + start, LEN), :] = h.astype(bf16)
            direct_copy(p).start()
            for piece in range(CHUNKS):
                relay_copy(0, p * CHUNKS + piece).start()

        each_passage(forward)

        def sent(p):
            direct_copy(p).wait_send()
            for piece in range(CHUNKS):
                relay_copy(0, p * CHUNKS + piece).wait_send()

        each_passage(sent)
        gain_sum[...] = jnp.zeros_like(gain_sum)

        def backward(p):
            start = pl.multiple_of(p * LEN, LEN)
            back_direct_copy(p).wait_recv()
            for piece in range(CHUNKS):
                back_relay_copy(2, p * CHUNKS + piece).wait_recv()
            dh = pool[pl.ds(DH_ROWS + start, LEN), :]
            pool[pl.ds(H_ROWS + start, LEN), :] = nt(dh, block(3)).astype(bf16)

            def pair(hp, carry):
                c = pair_columns(hp)
                q2 = pool[pl.ds(Q_ROWS + start, LEN), c]
                k2 = pool[pl.ds(K_ROWS + start, LEN), c]
                v2 = pool[pl.ds(V_ROWS + start, LEN), c]
                da = pool[pl.ds(H_ROWS + start, LEN), c].astype(f32)
                mixed = pool[pl.ds(O_ROWS + start, LEN), c].astype(f32)
                da = da * pool[pl.ds(IL_ROWS + start, LEN), c].astype(f32)
                product = da * mixed
                da = da.astype(bf16)
                one = jnp.ones_like(q2)
                zero = jnp.zeros_like(q2)
                dq = []
                dk = []
                dv = []
                for half in range(2):
                    mine = low_half if half == 0 else lane >= HEAD
                    spare = HEAD if half == 0 else 0
                    centre = -jnp.sum(jnp.where(mine, product, 0.0), axis=-1, keepdims=True)
                    centre_high = centre.astype(bf16)
                    centre_low = (centre - centre_high.astype(f32)).astype(bf16)
                    da_own = jnp.where(mine, da, zero)
                    da_ext = jnp.where(
                        lane == spare,
                        centre_high,
                        jnp.where(lane == spare + 1, centre_low, da_own),
                    )
                    at = pl.multiple_of((p * HEADS + hp * 2 + half) * 2 * LEN, 2 * LEN)
                    e = jnp.concatenate(
                        [wide[pl.ds(at, LEN), :], wide[pl.ds(at + LEN, LEN), :]], axis=1
                    )
                    ds = e * nt(da_ext, jnp.where(mine, v2, one)).astype(bf16)
                    dq.append(nn(ds, k2))
                    dk.append(nn(jnp.where(mine, q2, zero).T, ds))
                    dv.append(nn(da_own.T, e))
                pool[pl.ds(Q_ROWS + start, LEN), c] = jnp.where(low_half, dq[0], dq[1]).astype(bf16)
                pool[pl.ds(K_ROWS + start, LEN), c] = (
                    (dk[0] + dk[1]).T * (1.0 / log2_e)
                ).astype(bf16)
                pool[pl.ds(V_ROWS + start, LEN), c] = (dv[0] + dv[1]).T.astype(bf16)
                return carry

            lax.fori_loop(0, PAIRS, pair, 0)
            grad = (
                nt(pool[pl.ds(Q_ROWS + start, LEN), :], block(0))
                + nt(pool[pl.ds(K_ROWS + start, LEN), :], block(1))
                + nt(pool[pl.ds(V_ROWS + start, LEN), :], block(2))
            )
            x = pool[pl.ds(X_ROWS + start, LEN), :].astype(f32)
            inverse = inverse_rms(x)
            normed = x * inverse
            d_in = dh.astype(f32) + norm_back(normed, inverse, gain_row, grad)
            pool[pl.ds(H_ROWS + start, LEN), :] = d_in.astype(bf16)
            gain_sum[0:1, :] += jnp.sum(grad * normed, axis=0, keepdims=True)
            pool[pl.ds(X_ROWS + start, LEN), :] = (normed * gain_row).astype(bf16)
            for target in range(1, sections):
                out_enc_copy(target, p).start()
            local_copy(8 + p, rows(H_ROWS, start, chunk_len), o_enc.at[p]).start()

        each_passage(backward)
        outs = []
        for i, (left, right) in enumerate(
            ((X_ROWS, Q_ROWS), (X_ROWS, K_ROWS), (X_ROWS, V_ROWS), (O_ROWS, DH_ROWS))
        ):

            def columns(k, carry):
                c = pl.ds(pl.multiple_of(k * 256, 256), 256)
                pool[pl.ds(W_ROWS + i * D, D), c] = tn(
                    pool[left : left + ROWS, :], pool[right : right + ROWS, c]
                ).astype(bf16)
                return carry

            lax.fori_loop(0, 3, columns, 0)
            copy = local_copy(
                i, pool.at[pl.ds(W_ROWS + i * D, D)], o_dw.at[pl.ds(i * D, D)]
            )
            copy.start()
            outs.append(copy)
        for copy in outs:
            copy.wait()

        def finish(p):
            for target in range(1, sections):
                out_enc_copy(target, p).wait_send()
            local_copy(8 + p, rows(H_ROWS, p * LEN, chunk_len), o_enc.at[p]).wait()

        each_passage(finish)

    @pl.when(me == 1)
    def _():
        for c in weights_in(8):
            c.wait()
        gain_row = gain_ref[0:1, :]
        key_place = iota((1, LEN), 1)
        qk_copy().wait_recv()

        def tiles(b, p, base):
            return [
                pl.ds(pl.multiple_of(base + (3 * b + i) * ROWS + p * LEN, LEN), LEN)
                for i in range(3)
            ]

        def forward(p):
            start = pl.multiple_of(p * LEN, LEN)
            direct_copy(p).wait_recv()
            for piece in range(CHUNKS):
                relay_copy(2, p * CHUNKS + piece).wait_recv()
            h = pool[pl.ds(FF_H + start, LEN), :].astype(f32)
            a1 = (h * inverse_rms(h) * gain_row).astype(bf16)
            pool[pl.ds(FF_A + start, LEN), :] = a1
            acc[...] = h
            for b in range(4):
                r, slope = gelu_both(nn(a1, block(b)))
                r = r.astype(bf16)
                slope = slope.astype(bf16)
                for i, (at_r, at_s) in enumerate(zip(tiles(b, p, 0), tiles(b, p, GELU_ROWS))):
                    wide[at_r, :] = r[:, 256 * i : 256 * (i + 1)]
                    wide[at_s, :] = slope[:, 256 * i : 256 * (i + 1)]
                acc[...] += nn(r, block(4 + b))
            e = acc[...].astype(bf16)
            pool[pl.ds(FF_E + start, LEN), :] = e
            part = pl.ds(pl.multiple_of(p * 16, 16), 16)
            score = jnp.where(key_place < len_ref[p], nt(qk[part, :], e), masked_score)
            score = jnp.exp(score - jnp.max(score, axis=-1, keepdims=True))
            probs = score / jnp.sum(score, axis=-1, keepdims=True)
            cp[part, :] = probs
            mix[part, :] = nn(probs.astype(bf16), e).astype(bf16)
            mix_copy(p).start()

        each_passage(forward)
        each_passage(lambda p: mix_copy(p).wait_send())
        gain_sum[...] = jnp.zeros_like(gain_sum)
        g_copy().wait_recv()

        def backward(p):
            start = pl.multiple_of(p * LEN, LEN)
            part = pl.ds(pl.multiple_of(p * 16, 16), 16)
            e = pool[pl.ds(FF_E + start, LEN), :]
            probs = cp[part, :]
            d_probs = nt(gk[part, :], e)
            d_score = probs * (d_probs - jnp.sum(probs * d_probs, axis=-1, keepdims=True))
            d_score = d_score.astype(bf16)
            xs[part, :] = nn(d_score, e).astype(bf16)
            de = tn(d_score, qk[part, :]) + tn(probs.astype(bf16), gk[part, :])
            de = de.astype(bf16)
            pool[pl.ds(FF_E + start, LEN), :] = de
            for b in range(4):
                at = tiles(b, p, GELU_ROWS)
                slope = jnp.concatenate([wide[t, :] for t in at], axis=1)
                du = (nt(de, block(4 + b)) * slope.astype(f32)).astype(bf16)
                for i, t in enumerate(at):
                    wide[t, :] = du[:, 256 * i : 256 * (i + 1)]
                grad = nt(du, block(b))
                if b == 0:
                    acc[...] = grad
                else:
                    acc[...] += grad
            grad = acc[...]
            h = pool[pl.ds(FF_H + start, LEN), :].astype(f32)
            inverse = inverse_rms(h)
            normed = h * inverse
            dh = de.astype(f32) + norm_back(normed, inverse, gain_row, grad)
            gain_sum[0:1, :] += jnp.sum(grad * normed, axis=0, keepdims=True)
            pool[pl.ds(FF_H + start, LEN), :] = dh.astype(bf16)
            back_direct_copy(p).start()
            for piece in range(CHUNKS):
                back_relay_copy(0, p * CHUNKS + piece).start()

        each_passage(backward)
        x_copy().start()

        def term(b, carry):
            for i in range(3):
                t = 3 * b + i
                du = wide[pl.ds(pl.multiple_of(GELU_ROWS + t * ROWS, ROWS), ROWS), :]
                pool[
                    pl.ds(pl.multiple_of(W_ROWS + b * D, D), D), 256 * i : 256 * (i + 1)
                ] = tn(pool[FF_A : FF_A + ROWS, :], du).astype(bf16)
                r = wide[pl.ds(pl.multiple_of(t * ROWS, ROWS), ROWS), :]
                pool[pl.ds(pl.multiple_of(W_ROWS + (4 + b) * D + 256 * i, 256), 256), :] = tn(
                    r, pool[FF_E : FF_E + ROWS, :]
                ).astype(bf16)
            for k in (b, 4 + b):
                local_copy(
                    k,
                    pool.at[pl.ds(pl.multiple_of(W_ROWS + k * D, D), D)],
                    o_dw.at[pl.ds(pl.multiple_of(k * D, D), D)],
                ).start()
            return carry

        lax.fori_loop(0, 4, term, 0)

        def term_out(k, carry):
            local_copy(
                k,
                pool.at[pl.ds(pl.multiple_of(W_ROWS + k * D, D), D)],
                o_dw.at[pl.ds(pl.multiple_of(k * D, D), D)],
            ).wait()
            return carry

        lax.fori_loop(0, 8, term_out, 0)
        x_copy().wait_send()

        def sent(p):
            back_direct_copy(p).wait_send()
            for piece in range(CHUNKS):
                back_relay_copy(0, p * CHUNKS + piece).wait_send()

        each_passage(sent)

    def gathered_rows(own):
        copy = local_copy(20, small_ref, small.at[own])
        copy.start()
        for sender in range(sections):
            if sender != own:
                small_copy(sender, own).wait_recv()
        copy.wait()
        width = D // sections
        total = jnp.zeros((16, D), f32)
        for sender in range(sections):
            row, column = iota((256, D), 0), iota((256, D), 1)
            pick = jnp.where((column == row + width * sender) & (row < width), 1.0, 0.0)
            total = total + nn(small[sender], pick.astype(bf16))
        return total

    def moved(values, first, to):
        row, column = iota((16, 16), 0), iota((16, 16), 1)
        pick = (column - first == row - to) & (row >= to) & (row < to + GROUP)
        return nn(jnp.where(pick, 1.0, 0.0).astype(bf16), values)

    def packed(values):
        total = moved(values[0], 0, 0)
        for i, value in enumerate(values[1:]):
            total = total + moved(value, 0, GROUP * (i + 1))
        return total.astype(bf16)

    head_mask = (iota((64, D), 1) >> 6) == (iota((64, D), 0) & 15)

    def spread_heads(values):
        pick = jnp.where((iota((64, 16), 0) >> 4) == iota((64, 16), 1), 1.0, 0.0)
        return jnp.where(head_mask, nn(pick.astype(bf16), values), 0.0).astype(bf16)

    def join_heads(values):
        pick = jnp.where(iota((16, 64), 0) == (iota((16, 64), 1) >> 4), 1.0, 0.0)
        return nn(pick.astype(bf16), jnp.where(head_mask, values, 0.0).astype(bf16)).astype(bf16)

    def pass_on(copies, number):
        def step(index, carry):
            copies(number - 1, index).wait_recv()
            copies(number, index).start()
            return carry

        lax.fori_loop(0, GROUP * CHUNKS, step, 0)

    def passed(copies, number):
        def step(index, carry):
            copies(number, index).wait_send()
            return carry

        lax.fori_loop(0, GROUP * CHUNKS, step, 0)

    def fac_out():
        copy = local_copy(21, fac, o_fac)
        copy.start()
        copy.wait()

    @pl.when(me == 2)
    def _():
        weights = weights_in(6)
        x = moved(gathered_rows(2).astype(bf16), 0, 0)
        for c in weights:
            c.wait()
        gain_self = gain_ref[0:1, :]
        gain_cross = gain_ref[1:2, :]
        inverse_self = inverse_rms(x)
        normed_self = x * inverse_self
        a2 = (normed_self * gain_self).astype(bf16)
        sv = nn(a2, block(0)).astype(bf16)
        middle = x + nn(sv, block(1))
        inverse_cross = inverse_rms(middle)
        normed_cross = middle * inverse_cross
        a3 = (normed_cross * gain_cross).astype(bf16)
        cq = nn(a3, block(2)).astype(bf16)
        qk[...] = nt(spread_heads(cq), block(3)).astype(bf16)
        qk_copy().start()
        pass_on(relay_copy, 1)
        for p in range(GROUP):
            mix_copy(p).wait_recv()
        co = join_heads(nn(mix[...], block(4)))
        state[...] = (middle + nn(co, block(5))).astype(bf16)
        state_copy().start()
        state_back_copy().wait_recv()
        dy = state_back[...]
        dco = nt(dy, block(5)).astype(bf16)
        gk[...] = nt(spread_heads(dco), block(4)).astype(bf16)
        g_copy().start()
        pass_on(back_relay_copy, 2)
        x_copy().wait_recv()
        dcq = join_heads(nn(xs[...], block(3)))
        grad_cross = nt(dcq, block(2))
        dm = dy.astype(f32) + norm_back(normed_cross, inverse_cross, gain_cross, grad_cross)
        dm_low = dm.astype(bf16)
        dsv = nt(dm_low, block(1)).astype(bf16)
        grad_self = nt(dsv, block(0))
        d_in = dm + norm_back(normed_self, inverse_self, gain_self, grad_self)
        rows_out[1] = d_in.astype(bf16)
        gain_sum[...] = jnp.zeros_like(gain_sum)
        gain_sum[0:1, :] = jnp.sum(grad_self * normed_self, axis=0, keepdims=True)
        gain_sum[1:2, :] = jnp.sum(grad_cross * normed_cross, axis=0, keepdims=True)
        fac[0:16, :] = packed([a2, dsv, sv, dm_low])
        fac[16:32, :] = packed([a3, dcq, co, dy])
        fac[32:48, :] = packed([cq, dco])
        fac[48:112, :] = xs[...]
        fac[112:176, :] = mix[...]
        for target in range(sections):
            if target != 2:
                out_small_copy(target, 1).start()
        own = local_copy(22, rows_out.at[1], o_small.at[1])
        own.start()
        fac_out()
        own.wait()
        for target in range(sections):
            if target != 2:
                out_small_copy(target, 1).wait_send()
        passed(relay_copy, 1)
        passed(back_relay_copy, 2)
        qk_copy().wait_send()
        state_copy().wait_send()
        g_copy().wait_send()

    @pl.when(me == 3)
    def _():
        weights = weights_in(8)
        d_out = moved(gathered_rows(3).astype(bf16), GROUP, 0)
        d_low = d_out.astype(bf16)
        for c in weights:
            c.wait()
        gain_row = gain_ref[0:1, :]
        pass_on(relay_copy, 2)
        state_copy().wait_recv()
        y = state[...].astype(f32)
        inverse = inverse_rms(y)
        normed = y * inverse
        a4 = (normed * gain_row).astype(bf16)
        r4 = []
        du4 = []
        result = y
        grad = jnp.zeros((16, D), f32)
        for b in range(4):
            r, slope = gelu_both(nn(a4, block(b)))
            r4.append(r.astype(bf16))
            result = result + nn(r4[b], block(4 + b))
            du4.append((nt(d_low, block(4 + b)) * slope).astype(bf16))
            grad = grad + nt(du4[b], block(b))
        state_back[...] = (d_out + norm_back(normed, inverse, gain_row, grad)).astype(bf16)
        state_back_copy().start()
        pass_on(back_relay_copy, 1)
        rows_out[0] = result.astype(bf16)
        gain_sum[...] = jnp.zeros_like(gain_sum)
        gain_sum[0:1, :] = jnp.sum(grad * normed, axis=0, keepdims=True)
        fac[...] = jnp.zeros_like(fac)
        fac[0:16, :] = packed([a4, d_low, r4[0], r4[1]])
        fac[16:32, :] = packed([r4[2], r4[3], du4[0], du4[1]])
        fac[32:48, :] = packed([du4[2], du4[3]])
        for target in range(sections):
            if target != 3:
                out_small_copy(target, 0).start()
        own = local_copy(22, rows_out.at[0], o_small.at[0])
        own.start()
        fac_out()
        own.wait()
        for target in range(sections):
            if target != 3:
                out_small_copy(target, 0).wait_send()
        passed(relay_copy, 2)
        passed(back_relay_copy, 1)
        state_back_copy().wait_send()

    gains_out = local_copy(23, gain_sum, o_gain)
    gains_out.start()

    @pl.when(me != 2)
    def _():
        dynamic_small_copy(2).wait_send()
        remote(
            places.out_small[0] + me * 2 + 1, rows_out.at[1], o_small.at[1], 2
        ).wait_recv()

    @pl.when(me != 3)
    def _():
        dynamic_small_copy(3).wait_send()
        remote(places.out_small[0] + me * 2, rows_out.at[0], o_small.at[0], 3).wait_recv()

    @pl.when(me != 0)
    def _():
        def step(p, carry):
            dynamic_enc_copy(p).wait_send()
            remote(
                places.out_enc[0] + me * GROUP + p, rows(H_ROWS, p * LEN, chunk_len), o_enc.at[p], 0
            ).wait_recv()
            return carry

        lax.fori_loop(0, GROUP, step, 0)

    gains_out.wait()


def relay_call(sections, enc_in, lengths, small_in, gain_rows, weights):
    places = Places(sections)
    any_space = pl.BlockSpec(memory_space=pl.ANY)
    return pl.pallas_call(
        functools.partial(relay_kernel, sections, places),
        out_shape=(
            jax.ShapeDtypeStruct(enc_in.shape, bf16),
            jax.ShapeDtypeStruct((2, 16, D), bf16),
            jax.ShapeDtypeStruct((8 * D, D), bf16),
            jax.ShapeDtypeStruct((FAC_ROWS, D), bf16),
            jax.ShapeDtypeStruct((8, D), f32),
        ),
        in_specs=[
            pl.BlockSpec(memory_space=pltpu.SMEM),
            any_space,
            any_space,
            any_space,
            pl.BlockSpec(memory_space=pltpu.VMEM),
        ],
        out_specs=(any_space,) * 5,
        scratch_shapes=[
            pltpu.VMEM((POOL_ROWS, D), bf16),
            pltpu.VMEM((WIDE_ROWS, 256), bf16),
            pltpu.VMEM((LEN, D), f32),
            pltpu.VMEM((64, LEN), f32),
            pltpu.VMEM((sections, 16, 256), bf16),
            pltpu.VMEM((64, D), bf16),
            pltpu.VMEM((64, D), bf16),
            pltpu.VMEM((64, D), bf16),
            pltpu.VMEM((64, D), bf16),
            pltpu.VMEM((16, D), bf16),
            pltpu.VMEM((16, D), bf16),
            pltpu.VMEM((FAC_ROWS, D), bf16),
            pltpu.VMEM((2, 16, D), bf16),
            pltpu.VMEM((8, D), f32),
            pltpu.SemaphoreType.DMA((places.count,)),
            pltpu.SemaphoreType.DMA((places.count,)),
            pltpu.SemaphoreType.DMA((24,)),
        ],
        compiler_params=pltpu.CompilerParams(
            collective_id=0, has_side_effects=True, vmem_limit_bytes=63 * 1024 * 1024
        ),
    )(lengths, enc_in, small_in, weights, gain_rows)


def terms_two(total, fac):
    def part(tile, i):
        return fac[:, 16 * tile + GROUP * i : 16 * tile + GROUP * (i + 1)].reshape(-1, D)

    def outer(a, b):
        return lax.dot_general(a, b, (((0,), (0,)), ((), ())), preferred_element_type=f32)

    def by_head(tall, short):
        tall = tall.reshape(-1, GROUP, 16, D)[:, :, :HEADS].reshape(-1, HEADS, D)
        short = short.reshape(-1, HEADS, HEAD)
        return jnp.einsum("phd,phf->dhf", tall, short, preferred_element_type=f32).reshape(D, D)

    blocks = [
        outer(part(0, 0), part(0, 1)),
        outer(part(0, 2), part(0, 3)),
        outer(part(1, 0), part(1, 1)),
        by_head(fac[:, 48:112], part(2, 0)),
        by_head(fac[:, 112:176], part(2, 1)),
        outer(part(1, 2), part(1, 3)),
    ]
    zero = jnp.zeros((D, D), f32)
    return jnp.stack(blocks + [zero, zero])


def terms_three(total, fac):
    def part(i):
        return fac[:, GROUP * i : GROUP * (i + 1)].reshape(-1, D)

    def outer(a, b):
        return lax.dot_general(a, b, (((0,), (0,)), ((), ())), preferred_element_type=f32)

    blocks = [outer(part(0), part(6 + b)) for b in range(4)]
    blocks += [outer(part(2 + b), part(1)) for b in range(4)]
    return jnp.stack(blocks)


def terms_zero(total, fac):
    zero = jnp.zeros((4, D, D), f32)
    return jnp.concatenate([total[:4].astype(f32), zero], axis=0)


def terms_one(total, fac):
    return total.astype(f32)


def local(enc_in, lengths, dec_in, gains, weights, d_out):
    section = lax.axis_index("section")
    sections = lax.axis_size("section")
    width = dec_in.shape[1]
    small = jnp.concatenate([dec_in, d_out], axis=0)
    small = jnp.pad(small, ((0, 16 - 2 * GROUP), (0, 256 - width)))
    gain_rows = jnp.pad(gains[0].astype(f32), ((0, 6), (0, 0)))
    d_enc, rows_out, partial, fac, gain_part = relay_call(
        sections, enc_in, lengths, small, gain_rows, weights[0].reshape(8 * D, D)
    )
    fac = lax.all_gather(fac, "dp", axis=0)
    total_gains = lax.psum(gain_part, "dp")[:2]
    total = lax.psum(partial.reshape(8, D, D), "dp")
    total_weights = lax.switch(
        section, [terms_zero, terms_one, terms_two, terms_three], total, fac
    )
    own = lax.dynamic_slice(rows_out, (0, 0, section * width), (2, GROUP, width))
    return (own[0], d_enc, own[1], total_gains[None], total_weights[None])


def solution(mesh):
    in_specs = (
        P("dp", "section", None),
        P("dp"),
        P("dp", "section"),
        P("section", None, None),
        P("section", None, None, None),
        P("dp", "section"),
    )
    out_specs = (
        P("dp", "section"),
        P("dp", "section", None),
        P("dp", "section"),
        P("section", None, None),
        P("section", None, None, None),
    )
    return jax.shard_map(local, mesh=mesh, in_specs=in_specs, out_specs=out_specs, check_vma=False)
```

time: 1980 us -> 491 us (0.25)
  starting transfers between devices: 460 us -> 0.08 us
  waiting for transfers between devices: 608 us -> 214 us
  matrix products: 271 us -> 9.74 us
  other arithmetic: 232 us -> 2.6 us
  Pallas kernels: 0 us -> 191 us
  local copies, waits for them, and re-layouts: 172 us -> 23.1 us
  blocking collectives: 149 us -> 26.7 us
  loops' own time: 48.9 us -> 0.59 us
    ppermute x28 -> x0, starting transfers between devices: 460 us -> none  [from_behind(): return lax.ppermute(block, axis, route)]
    dot_general x175 -> x6, matrix products: 271 us -> 9.74 us  [the longest x4 7.65 us: outer(): lax.dot_general(a, b, (((0,), (0,)), ((), ())), preferred_element_type=f32)]
    pallas_call x0 -> x1, Pallas kernels: none -> 191 us  [relay_call(): pl.pallas_call(functools.partial(relay_kernel, sections, places), out_sha...]
    psum x1, waiting for transfers between devices: 375 us -> 197 us  [local(): total = lax.psum(partial.reshape(8, D, D), 'dp')]
    ppermute x28 -> x0, waiting for transfers between devices: 122 us -> none  [from_behind(): return lax.ppermute(block, axis, route)]
    add x21 -> x0, other arithmetic: 112 us -> none  [the longest x7 111 us: backward_tick(): sum_weights = sum_weights + term_stack]
    psum x1, blocking collectives: 133 us -> 26.7 us  [local(): total_gains = lax.psum(gain_part, 'dp')[:2]]
    another operation x109 -> x1, local copies, waits for them, and re-layouts: 51.7 us -> 2.49 us  [terms_two(): return jnp.stack(blocks + [zero, zero])]
  transfers between devices with their start and end apart: 33 -> 2, of which waited for: 12 -> 2; matrix products, arithmetic and copies ran while one was open for 7% -> 0% of each run, Pallas kernels for 0% -> 0%
where the time goes in v1:
time: 491 us; the launch traced here: 483 us
  waiting for transfers between devices  214 us (44%)
  Pallas kernels  191 us (39%)
  blocking collectives  26.7 us (5%)
  local copies, waits for them, and re-layouts  23.1 us (5%)
  between operations  14.6 us (3%)
  matrix products  9.74 us (2%)
    psum x1, waiting for transfers between devices, local(): total = lax.psum(partial.reshape(8, D, D), 'dp')  197 us
    pallas_call x1, Pallas kernels, relay_call(): pl.pallas_call(functools.partial(relay_kernel, sections, places), out_sha...  191 us
    psum x1, blocking collectives, local(): total_gains = lax.psum(gain_part, 'dp')[:2]  26.7 us
    all_gather x1, waiting for transfers between devices, local(): fac = lax.all_gather(fac, 'dp', axis=0)  16.5 us
  transfers between devices with their start and end apart: 2, of which 2 were waited for; matrix products, arithmetic and copies ran while one was open for 0% of the time, Pallas kernels for 0%

profile of v1, /device:TPU:4, one launch (start us, length us, event | category | flops | bytes accessed | tf_op | source)
XLA Modules:
  0.0 482.8 jit_solution(58730214654542466)
XLA Ops:
  7.2 1.3 pad_convert_fusion.gain_ref
  8.5 1.3 fusion.33.small_ref
  9.8 191.0 %shard_map.101 = (bf16[4,128,768]{2,1,0:T(8,128)(2,1)}, bf16[2,16,768]{2,1,0:T(8,128)(2,1)}, bf16[6144,768]{1,0:T(8,128)(2,1)}, bf16[176,768]{1,0:T(8,128)(2,1)}, f32[8,768]{1,0:T(8,128)}) custom-call(s32[4]{0:T(128)} %len_ref.1, bf16[4,128,768]{2,1,0:T(8,128)(2,1)} %enc_ref.1, bf16[16,256]{1,0:T(8,128)(2,1)} %fusion.33.small_ref, ...), custom_call_target="tpu_custom_call" | custom-call | tf_op jit(solution)/shard_map/pallas_call | solution.py:793
  200.9 0.7 all-reduce.4.cloned.1.call-update
  201.6 26.7 %psum.20 = f32[8,768]{1,0:T(8,128)S(1)} all-reduce(f32[8,768]{1,0:T(8,128)} %get-tuple-element.22), channel_id=1, replica_groups=mesh['section'=4,'dp'=8] {'dp'}, use_global_device_ids=true, to_apply=%region_0.1 | all-reduce | flops 6144 | bytes 49152 | tf_op jit(solution)/shard_map/psum | solution.py:891
  228.3 1.4 dynamic-slice_bitcast_fusion
  229.7 0.6 slice_bitcast_fusion
  230.3 16.5 %all-gather.3.cloned.1.call-done = bf16[1408,768]{1,0:T(8,128)(2,1)} async-done(((bf16[176,768]{1,0:T(8,128)(2,1)}), bf16[1408,768]{1,0:T(8,128)(2,1)}) %all-gather.3.cloned.1.call-update) | async-done | bytes 2162704 | tf_op jit(solution)/shard_map/all_gather | solution.py:890
  246.8 197.3 %all-reduce.4.cloned.1.call-done = bf16[8,768,768]{2,1,0:T(8,128)(2,1)} async-done(((bf16[8,768,768]{2,1,0:T(8,128)(2,1)}), bf16[8,768,768]{2,1,0:T(8,128)(2,1)}) %all-reduce.4.cloned.1.call-update) | async-done | bytes 9437200 | tf_op jit(solution)/shard_map/psum | solution.py:892
  444.0 29.4 %conditional.1 = (f32[1,8,768,768]{3,2,1,0:T(8,128)}) conditional(s32[]{:T(128)} %clamp.3, bf16[8,768,768]{2,1,0:T(8,128)(2,1)} %all-reduce.4.cloned.1.call-done, bf16[8,768,768]{2,1,0:T(8,128)(2,1)} %all-reduce.4.cloned.1.call-done, bf16[8,176,768]{2,1,0:T(8,128)(2,1)} %bitcast.74, ...), branch_computations={%region_2.3_spmd, %region_3.4_spmd, %region_4.5_spmd, %region_5.6_... | conditional | flops 301989888 | bytes 53968904 | solution.py:893
  444.3 1.5 fusion.34
  445.8 1.9 bitcast_dynamic-update-slice_fusion.3
  447.7 1.9 bitcast_dynamic-update-slice_fusion.2
  449.6 1.9 bitcast_dynamic-update-slice_fusion.1
  451.5 1.5 fusion.35
  453.0 0.4 copy.34
  453.5 0.5 copy.35
  454.0 1.0 reshape.34
  454.9 0.1 reshape.8
  455.1 1.6 fusion.2
  456.6 2.0 copy.23
  458.6 3.2 constant_dynamic-update-slice_fusion.1
  461.8 0.4 copy.37
  462.3 0.5 copy.38
  462.8 0.1 reshape.38
  462.9 0.1 reshape.36
  463.1 0.5 fusion
  463.6 2.0 copy.24
  465.5 3.2 constant_dynamic-update-slice_fusion
  468.8 1.9 bitcast_dynamic-update-slice_fusion
  470.7 2.5 broadcast_dynamic-update-slice_fusion
  473.4 2.1 copy.124
  (5 shorter events, 0.2 us)
Async XLA Ops:
  7.2 239.6 %all-gather.3.cloned.1.call-start = ((), (), s32[]{:S(2)}) async-start(), calls=%async_computation.1 | async-start | bytes 2433024 | tf_op jit(solution)/shard_map/all_gather | solution.py:890
  200.9 243.1 %all-reduce.4.cloned.1.call-start = ((), (), s32[]{:S(2)}) async-start(), calls=%async_computation | async-start | bytes 18874368 | tf_op jit(solution)/shard_map/psum | solution.py:892
Sparse Core Ops, SparseCore 0:
  201.0 45.7 all-gather.2
  249.1 194.8 all-reduce.3
